TPU v7x, 256 devices: a whole 4x4x8 slice. The times are simulated.
256 devices in a mesh: seq: 64 (over y, z, core), dp: 4 (over x).
Axes of the slice: x: 4, y: 4, z: 8, core: 2. Of those that a mesh axis runs over, the one named last changes fastest.
Arguments:
- features: bfloat16 [4, 131072, 192], P('dp', 'seq'), may hold values from -6 to 6
- grad_out: bfloat16 [4, 131072, 192], P('dp', 'seq'), may hold values from -6 to 6
- norm_gain: float32 [192], replicated, may hold values from 0.5 to 4
- w_qkv: bfloat16 [192, 576], replicated, may hold values from -0.4375 to 0.4375
- w_proj: bfloat16 [192, 192], replicated, may hold values from -0.4375 to 0.4375
- to_hilbert: int32 [4, 131072], P('dp', 'seq'), may hold values from 0 to 131071, as said below
- to_zorder: int32 [4, 131072], P('dp', 'seq'), may hold values from 0 to 131071, as said below
- counts: int32 [4, 128], P('dp', 'seq'), may hold values from 256 to 1024
Outputs:
- block_out: bfloat16 [4, 131072, 192], P('dp', 'seq')
- grad_features: bfloat16 [4, 131072, 192], P('dp', 'seq')
- grad_qkv: float32 [192, 576], replicated
- grad_proj: float32 [192, 192], replicated
- grad_gain: float32 [192], replicated
Inputs may be any that keep to these rules, and one draw needn't show every extreme that they name: to_hilbert[s] is a permutation; each point's Hilbert position lies on the same index of seq as its Z position or on an adjacent one; at most 1024 points go from one index to an adjacent one, and in every slab exactly 1024 go from index 0 to index 1 and 1024 from index 1 to index 0. to_zorder[s] is the inverse permutation of to_hilbert[s].
All inputs are finite; a program needn't handle non-finite values.
Results may differ from a plain program's by a relative error of at most 0.006.
The roundings to bfloat16 on the way count: a program that leaves them out, or rounds other values in their place, can miss the bound.
Values may be sent and summed in bfloat16 or wider, within the bound.
A program may use at most 128 MiB of HBM per device.

v0:
```python
import jax
import jax.numpy as jnp
from jax import lax
from jax.sharding import PartitionSpec as P

HEADS = 3
PATCH = 1024


EPS = 1e-05
NEG = -1e30


def extended(x, sides, width):
    for axis, dim in sides:
        peers, length = (lax.axis_size(axis), x.shape[dim])
        up = [(i, (i + 1) % peers) for i in range(peers - 1)]
        down = [(j, i) for i, j in up]
        last = lax.slice_in_dim(x, length - width, length, axis=dim)
        leading = lax.slice_in_dim(x, 0, width, axis=dim)
        before = lax.ppermute(last, axis, up)
        after = lax.ppermute(leading, axis, down)
        x = jnp.concatenate([before, x, after], axis=dim)
    return x


def normalize(row_block, gain_vec):
    as_float = row_block.astype(jnp.float32)
    center = as_float - jnp.mean(as_float, axis=-1, keepdims=True)
    inv_std = lax.rsqrt(jnp.mean(center * center, axis=-1, keepdims=True) + EPS)
    unit_rows = center * inv_std
    return (unit_rows, inv_std, (unit_rows * gain_vec).astype(jnp.bfloat16))


def split_heads(qkv_rows, head_count):
    row_count = qkv_rows.shape[0]
    feat_width = qkv_rows.shape[1] // 3
    head_size = feat_width // head_count
    queries = qkv_rows[:, :feat_width].reshape(row_count, head_count, head_size)
    keys_h = qkv_rows[:, feat_width : 2 * feat_width].reshape(row_count, head_count, head_size)
    values_h = qkv_rows[:, 2 * feat_width :].reshape(row_count, head_count, head_size)
    return (queries, keys_h, values_h)


def probabilities(queries, keys_h, live_count, score_scale):
    scores = (
        jnp.einsum("qhd,khd->hqk", queries, keys_h, preferred_element_type=jnp.float32)
        * score_scale
    )
    live_flag = jnp.arange(keys_h.shape[0]) < live_count
    scores = jnp.where(live_flag[None, None, :], scores, NEG)
    highest = jnp.max(scores, axis=-1, keepdims=True)
    weights = jnp.exp(scores - highest)
    attn_probs = weights / jnp.sum(weights, axis=-1, keepdims=True)
    return (attn_probs, live_flag.astype(jnp.float32)[:, None])


def route_plan(send_key, recv_key, my_index, per_dev, spill):
    send_order = jnp.argsort(send_key, stable=True)
    sent_left = jnp.sum((send_key < my_index * per_dev).astype(jnp.int32))
    source = recv_key // per_dev - my_index + 1
    group_order = jnp.argsort(source, stable=True)
    position = (
        jnp.zeros((per_dev,), jnp.int32).at[group_order].set(jnp.arange(per_dev, dtype=jnp.int32))
    )
    from_left = jnp.sum((source == 0).astype(jnp.int32))
    from_self = jnp.sum((source == 1).astype(jnp.int32))
    stream_idx = jnp.where(
        source == 0,
        spill - from_left + position,
        jnp.where(
            source == 1,
            spill + sent_left + position - from_left,
            spill + per_dev + position - from_left - from_self,
        ),
    )
    return (send_order, stream_idx)


def shards(features, grad_out, norm_gain, w_qkv, w_proj, to_hilbert, to_zorder, counts):
    per_dev = features.shape[1]
    feat_width = features.shape[2]
    spill = per_dev // 2
    patches = per_dev // PATCH
    score_scale = (feat_width // HEADS) ** (-0.5)
    my_index = lax.axis_index("seq")
    hil_pos = to_hilbert[0]
    zor_pos = to_zorder[0]
    send_fwd, place_fwd = route_plan(hil_pos, zor_pos, my_index, per_dev, spill)
    send_back, place_back = route_plan(zor_pos, hil_pos, my_index, per_dev, spill)

    def by_patch(array_in):
        return array_in.reshape((patches, PATCH) + array_in.shape[1:])

    x_hil = extended(features[0][send_fwd], (("seq", 0),), spill)[place_fwd]
    unit_rows, inv_std, normed = normalize(x_hil, norm_gain)
    live_counts = counts[0]

    def patch_forward(patch_items):
        x_patch, normed_patch, live_count = patch_items
        qkv_rows = jnp.dot(normed_patch, w_qkv, preferred_element_type=jnp.float32).astype(
            jnp.bfloat16
        )
        queries, keys_h, values_h = split_heads(qkv_rows, HEADS)
        attn_probs, live_mask = probabilities(queries, keys_h, live_count, score_scale)
        attended = jnp.einsum(
            "hqk,khd->qhd",
            attn_probs.astype(jnp.bfloat16),
            values_h,
            preferred_element_type=jnp.float32,
        )
        attended = attended.reshape(PATCH, feat_width).astype(jnp.bfloat16)
        branch = jnp.dot(attended, w_proj, preferred_element_type=jnp.float32)
        block_rows = (x_patch.astype(jnp.float32) + live_mask * branch).astype(jnp.bfloat16)
        return (block_rows, qkv_rows, attended)

    y_hil, qkv_all, attn_all = lax.map(
        patch_forward, (by_patch(x_hil), by_patch(normed), live_counts)
    )
    y_hil = y_hil.reshape(per_dev, feat_width)
    y_zor = extended(y_hil[send_back], (("seq", 0),), spill)[place_back]
    g_hil = extended(grad_out[0][send_fwd], (("seq", 0),), spill)[place_fwd]

    def patch_backward(totals, patch_items):
        g_patch, unit_patch, inv_patch, normed_patch, qkv_rows, attended, live_count = patch_items
        queries, keys_h, values_h = split_heads(qkv_rows, HEADS)
        attn_probs, live_mask = probabilities(queries, keys_h, live_count, score_scale)
        probs_bf16 = attn_probs.astype(jnp.bfloat16)
        g_masked = (g_patch.astype(jnp.float32) * live_mask).astype(jnp.bfloat16)
        grad_proj = jnp.dot(attended.T, g_masked, preferred_element_type=jnp.float32)
        d_attn = jnp.dot(g_masked, w_proj.T, preferred_element_type=jnp.float32).astype(
            jnp.bfloat16
        )
        d_attn = d_attn.reshape(PATCH, HEADS, -1)
        d_probs = jnp.einsum("qhd,khd->hqk", d_attn, values_h, preferred_element_type=jnp.float32)
        d_values = jnp.einsum(
            "hqk,qhd->khd", probs_bf16, d_attn, preferred_element_type=jnp.float32
        )
        row_delta = jnp.sum(attn_probs * d_probs, axis=-1, keepdims=True)
        d_scores = (attn_probs * (d_probs - row_delta) * score_scale).astype(jnp.bfloat16)
        d_queries = jnp.einsum("hqk,khd->qhd", d_scores, keys_h, preferred_element_type=jnp.float32)
        d_keys = jnp.einsum("hqk,qhd->khd", d_scores, queries, preferred_element_type=jnp.float32)
        d_qkv = jnp.concatenate(
            [
                d_queries.reshape(PATCH, feat_width),
                d_keys.reshape(PATCH, feat_width),
                d_values.reshape(PATCH, feat_width),
            ],
            axis=1,
        ).astype(jnp.bfloat16)
        grad_qkv = jnp.dot(normed_patch.T, d_qkv, preferred_element_type=jnp.float32)
        d_normed = jnp.dot(d_qkv, w_qkv.T, preferred_element_type=jnp.float32)
        grad_gain = jnp.sum(unit_patch * d_normed, axis=0)
        d_unit = d_normed * norm_gain
        d_rows = inv_patch * (
            d_unit
            - jnp.mean(d_unit, axis=-1, keepdims=True)
            - unit_patch * jnp.mean(d_unit * unit_patch, axis=-1, keepdims=True)
        )
        grad_rows = (g_patch.astype(jnp.float32) + d_rows).astype(jnp.bfloat16)
        return ((totals[0] + grad_qkv, totals[1] + grad_proj, totals[2] + grad_gain), grad_rows)

    start_totals = (
        jnp.zeros(w_qkv.shape, jnp.float32),
        jnp.zeros(w_proj.shape, jnp.float32),
        jnp.zeros(norm_gain.shape, jnp.float32),
    )
    local_totals, dx_hil = lax.scan(
        patch_backward,
        start_totals,
        (
            by_patch(g_hil),
            by_patch(unit_rows),
            by_patch(inv_std),
            by_patch(normed),
            qkv_all,
            attn_all,
            live_counts,
        ),
    )
    dx_hil = dx_hil.reshape(per_dev, feat_width)
    grad_qkv, grad_proj, grad_gain = lax.psum(
        (local_totals[0], local_totals[1], local_totals[2]), ("seq", "dp")
    )
    dx_zor = extended(dx_hil[send_back], (("seq", 0),), spill)[place_back]
    return (y_zor[None], dx_zor[None], grad_qkv, grad_proj, grad_gain)


def solution(mesh):
    in_specs = (
        P("dp", "seq", None),
        P("dp", "seq", None),
        P(),
        P(),
        P(),
        P("dp", "seq"),
        P("dp", "seq"),
        P("dp", "seq"),
    )
    out_specs = (P("dp", "seq", None), P("dp", "seq", None), P(), P(), P())
    return jax.shard_map(shards, mesh=mesh, in_specs=in_specs, out_specs=out_specs, check_vma=False)
```

profile of v0, /device:TPU:1, one launch (start us, length us, event | category | flops | bytes accessed | tf_op | source)
XLA Modules:
  0.0 586.8 jit_solution(18007666743966886377)
XLA Ops:
  7.2 5.7 sort.59
  14.4 7.5 %gather_fusion = bf16[2048,192]{1,0:T(8,128)(2,1)S(1)} fusion(bf16[2048,192]{1,0:T(8,128)(2,1)S(1)} %bitcast.207, s32[2048]{0:T(1024)S(1)} %fusion.90), kind=kCustom, calls=%fused_computation | custom fusion | bytes 1581056 | tf_op jit(solution)/shard_map/gather | solution.py:95
  22.9 4.9 collective-permute-start
  27.8 2.3 collective-permute-start.1
  30.7 7.5 %gather_fusion.4 = bf16[2048,192]{1,0:T(8,128)(2,1)S(1)} fusion(bf16[2048,192]{1,0:T(8,128)(2,1)S(1)} %bitcast.205, s32[2048]{0:T(1024)S(1)} %fusion.90), kind=kCustom, calls=%fused_computation.4 | custom fusion | bytes 1581056 | tf_op jit(solution)/shard_map/gather | solution.py:122
  39.3 3.3 collective-permute-start.4
  42.6 1.9 collective-permute-start.5
  46.6 5.0 sort.60
  52.8 5.0 sort.61
  58.4 5.0 sort.62
  64.7 8.0 %scatter_custom_fusion = s32[2048]{0:T(1024)S(1)} fusion(s32[2048]{0:T(1024)S(1)} %compare_select_fusion.4, s32[2048]{0:T(1024)S(1)} %iota.35, s32[]{:T(128)} %constant.87.clone.1), kind=kCustom, calls=%fused_computation.154 | custom fusion | bytes 8196 | tf_op jit(solution)/shard_map/scatter | solution.py:64
  72.8 8.6 %scatter_custom_fusion.1 = s32[2048]{0:T(1024)} fusion(s32[2048]{0:T(1024)S(1)} %compare_select_fusion.1, s32[2048]{0:T(1024)S(1)} %iota.38, s32[]{:T(128)} %constant.87.clone.1), kind=kCustom, calls=%fused_computation.157 | custom fusion | bytes 8196 | tf_op jit(solution)/shard_map/scatter | solution.py:64
  83.9 1.9 pad_maximum_fusion.3
  85.8 7.5 %gather_fusion.1 = bf16[2048,192]{1,0:T(8,128)(2,1)S(1)} fusion(bf16[4096,192]{1,0:T(8,128)(2,1)S(1)} %pad_maximum_fusion.3, s32[2048]{0:T(1024)S(1)} %fusion.91), kind=kCustom, calls=%fused_computation.1 | custom fusion | bytes 1581056 | tf_op jit(solution)/shard_map/gather | solution.py:95
  96.9 2.5 subtract_multiply_fusion
  101.0 37.0 %while.31 = (s32[]{:T(128)}, bf16[2,1024,192]{1,2,0:T(8,128)(2,1)}, bf16[2,1024,576]{1,2,0:T(8,128)(2,1)}, bf16[2,1024,192]{1,2,0:T(8,128)(2,1)S(1)}, bf16[2,102...) while((s32[]{:T(128)}, bf16[2,1024,192]{1,2,0:T(8,128)(2,1)}, ...), condition=%wide.region_11.12_spmd, body=%wide.region_8.11_spmd.sunk | while | flops 1127746560 | bytes 40619188 | solution.py:117
  101.0 1.6 bitcast_dynamic-update-slice_fusion.2
  103.9 7.5 %fusion.171 = (f32[3,1024]{1,0:T(4,128)S(1)}, f32[3,1024,1024]{1,2,0:T(8,128)}) fusion(pred[1024]{0:T(1024)(128)(4,1)S(1)} %get-tuple-element.475, bf16[1024,3,64]{0,2,1:T(8,128)(2,1)S(1)} %bitcast.218, bf16[1024,3,64]{0,2,1:T(8,128)(2,1)S(1)} %bitcast.217), kind=kOutput, calls=%fused_computation.160.clone.1 | convolution fusion | flops 415237120 | bytes 13382656 | tf_op jit(solution)/shard_map/while/body/eval_jaxpr/sub | solution.py:53
  111.4 5.9 fusion.172
  122.3 7.5 %fusion.171 = (f32[3,1024]{1,0:T(4,128)S(1)}, f32[3,1024,1024]{1,2,0:T(8,128)}) fusion(pred[1024]{0:T(1024)(128)(4,1)S(1)} %get-tuple-element.475, bf16[1024,3,64]{0,2,1:T(8,128)(2,1)S(1)} %bitcast.218, bf16[1024,3,64]{0,2,1:T(8,128)(2,1)S(1)} %bitcast.217), kind=kOutput, calls=%fused_computation.160.clone.1 | convolution fusion | flops 415237120 | bytes 13382656 | tf_op jit(solution)/shard_map/while/body/eval_jaxpr/sub | solution.py:53
  129.9 5.9 fusion.172
  139.2 1.9 pad_maximum_fusion.5
  141.1 9.0 %gather_fusion.5 = bf16[2048,192]{1,0:T(8,128)(2,1)} fusion(bf16[4096,192]{1,0:T(8,128)(2,1)S(1)} %pad_maximum_fusion.5, s32[2048]{0:T(1024)S(1)} %fusion.91), kind=kCustom, calls=%fused_computation.5 | custom fusion | bytes 1581056 | tf_op jit(solution)/shard_map/gather | solution.py:122
  152.5 132.6 %while.32 = (s32[]{:T(128)}, f32[192,576]{1,0:T(8,128)}, f32[192,192]{1,0:T(8,128)}, f32[192]{0:T(256)S(1)}, bf16[2,1024,192]{1,2,0:T(8,128)(2,1)}, /*index=5*/b...) while((s32[]{:T(128)}, f32[192,576]{1,0:T(8,128)}, ...), condition=%wide.region_25.26_spmd.clone, body=%wide.region_18.25_spmd.clone.sunk | while | flops 2692262912 | bytes 129294584 | solution.py:168
  155.2 7.5 %fusion.191 = (f32[3,1024]{1,0:T(4,128)S(1)}, f32[3,1024,1024]{1,2,0:T(8,128)}) fusion(pred[1024]{0:T(1024)(128)(4,1)S(1)} %get-tuple-element.498, bf16[1024,3,64]{0,2,1:T(8,128)(2,1)S(1)} %bitcast.212, bf16[1024,3,64]{0,2,1:T(8,128)(2,1)S(1)} %bitcast.214), kind=kOutput, calls=%fused_computation.162.clone.1 | convolution fusion | flops 415237120 | bytes 13382656 | tf_op jit(solution)/shard_map/while/body/eval_jaxpr/sub | solution.py:53
  163.0 6.3 %fusion.193 = f32[3,1024,1024]{1,2,0:T(8,128)} fusion(bf16[1024,3,64]{0,2,1:T(8,128)(2,1)S(1)} %bitcast.209, bf16[1024,3,64]{0,2,1:T(8,128)(2,1)S(1)} %bitcast.208), kind=kOutput, calls=%fused_computation.167.clone.1 | convolution fusion | flops 402653184 | bytes 13369344 | tf_op jit(solution)/shard_map/while/body/eval_jaxpr/qhd,khd->hqk/dot_general | solution.py:135
  169.3 18.4 %fusion.195 = bf16[3,64,1024]{2,1,0:T(8,128)(2,1)} fusion(bf16[1024,3,64]{0,2,1:T(8,128)(2,1)S(1)} %bitcast.215, f32[3,1024,1024]{1,2,0:T(8,128)} %fusion.193, f32[3,1024,1024]{1,2,0:T(8,128)} %get-tuple-element.501, f32[3,1024]{1,0:T(4,128)S(1)} %get-tuple-element.502), kind=kOutput, calls=%fused_computation.53.clone.1 | convolution fusion | flops 424873984 | bytes 25964544 | tf_op jit(solution)/shard_map/while/body/eval_jaxpr/hqk,khd->qhd/dot_general | solution.py:141
  187.7 17.8 %fusion.194 = bf16[3,64,1024]{2,1,0:T(8,128)(2,1)S(1)} fusion(bf16[1024,3,64]{0,2,1:T(8,128)(2,1)S(1)} %bitcast.213, f32[3,1024,1024]{1,2,0:T(8,128)} %fusion.193, f32[3,1024,1024]{1,2,0:T(8,128)} %get-tuple-element.501, f32[3,1024]{1,0:T(4,128)S(1)} %get-tuple-element.502), kind=kOutput, calls=%fused_computation.54.clone.1 | convolution fusion | flops 424873984 | bytes 25964544 | tf_op jit(solution)/shard_map/while/body/eval_jaxpr/hqk,qhd->khd/dot_general | solution.py:142
  205.6 6.8 %fusion.192 = bf16[3,64,1024]{2,1,0:T(8,128)(2,1)S(1)} fusion(bf16[1024,3,64]{0,2,1:T(8,128)(2,1)S(1)} %bitcast.210, f32[3,1024,1024]{1,2,0:T(8,128)} %get-tuple-element.501, f32[3,1024]{1,0:T(4,128)S(1)} %get-tuple-element.502), kind=kOutput, calls=%fused_computation.55.clone.1 | convolution fusion | flops 409141248 | bytes 13381632 | tf_op jit(solution)/shard_map/while/body/eval_jaxpr/hqk,qhd->khd/dot_general | solution.py:136
  215.1 2.7 convolution_add_fusion.4
  221.5 7.5 %fusion.191 = (f32[3,1024]{1,0:T(4,128)S(1)}, f32[3,1024,1024]{1,2,0:T(8,128)}) fusion(pred[1024]{0:T(1024)(128)(4,1)S(1)} %get-tuple-element.498, bf16[1024,3,64]{0,2,1:T(8,128)(2,1)S(1)} %bitcast.212, bf16[1024,3,64]{0,2,1:T(8,128)(2,1)S(1)} %bitcast.214), kind=kOutput, calls=%fused_computation.162.clone.1 | convolution fusion | flops 415237120 | bytes 13382656 | tf_op jit(solution)/shard_map/while/body/eval_jaxpr/sub | solution.py:53
  229.3 6.3 %fusion.193 = f32[3,1024,1024]{1,2,0:T(8,128)} fusion(bf16[1024,3,64]{0,2,1:T(8,128)(2,1)S(1)} %bitcast.209, bf16[1024,3,64]{0,2,1:T(8,128)(2,1)S(1)} %bitcast.208), kind=kOutput, calls=%fused_computation.167.clone.1 | convolution fusion | flops 402653184 | bytes 13369344 | tf_op jit(solution)/shard_map/while/body/eval_jaxpr/qhd,khd->hqk/dot_general | solution.py:135
  235.6 18.4 %fusion.195 = bf16[3,64,1024]{2,1,0:T(8,128)(2,1)} fusion(bf16[1024,3,64]{0,2,1:T(8,128)(2,1)S(1)} %bitcast.215, f32[3,1024,1024]{1,2,0:T(8,128)} %fusion.193, f32[3,1024,1024]{1,2,0:T(8,128)} %get-tuple-element.501, f32[3,1024]{1,0:T(4,128)S(1)} %get-tuple-element.502), kind=kOutput, calls=%fused_computation.53.clone.1 | convolution fusion | flops 424873984 | bytes 25964544 | tf_op jit(solution)/shard_map/while/body/eval_jaxpr/hqk,khd->qhd/dot_general | solution.py:141
  254.0 17.8 %fusion.194 = bf16[3,64,1024]{2,1,0:T(8,128)(2,1)S(1)} fusion(bf16[1024,3,64]{0,2,1:T(8,128)(2,1)S(1)} %bitcast.213, f32[3,1024,1024]{1,2,0:T(8,128)} %fusion.193, f32[3,1024,1024]{1,2,0:T(8,128)} %get-tuple-element.501, f32[3,1024]{1,0:T(4,128)S(1)} %get-tuple-element.502), kind=kOutput, calls=%fused_computation.54.clone.1 | convolution fusion | flops 424873984 | bytes 25964544 | tf_op jit(solution)/shard_map/while/body/eval_jaxpr/hqk,qhd->khd/dot_general | solution.py:142
  271.9 6.8 %fusion.192 = bf16[3,64,1024]{2,1,0:T(8,128)(2,1)S(1)} fusion(bf16[1024,3,64]{0,2,1:T(8,128)(2,1)S(1)} %bitcast.210, f32[3,1024,1024]{1,2,0:T(8,128)} %get-tuple-element.501, f32[3,1024]{1,0:T(4,128)S(1)} %get-tuple-element.502), kind=kOutput, calls=%fused_computation.55.clone.1 | convolution fusion | flops 409141248 | bytes 13381632 | tf_op jit(solution)/shard_map/while/body/eval_jaxpr/hqk,qhd->khd/dot_general | solution.py:136
  281.3 2.8 convolution_add_fusion.4
  286.7 7.8 %gather_fusion.6 = bf16[2048,192]{1,0:T(8,128)(2,1)S(1)} fusion(bf16[2048,192]{1,0:T(8,128)(2,1)S(1)} %bitcast.206, s32[2048]{0:T(1024)S(1)} %copy-done.20), kind=kCustom, calls=%fused_computation.6 | custom fusion | bytes 1581056 | tf_op jit(solution)/shard_map/gather | solution.py:185
  295.5 3.6 collective-permute-start.6
  299.2 1.9 collective-permute-start.7
  302.8 7.5 %gather_fusion.2 = bf16[2048,192]{1,0:T(8,128)(2,1)S(1)} fusion(bf16[2048,192]{1,0:T(8,128)(2,1)S(1)} %bitcast.204, s32[2048]{0:T(1024)S(1)} %copy-done.20), kind=kCustom, calls=%fused_computation.2 | custom fusion | bytes 1581056 | tf_op jit(solution)/shard_map/gather | solution.py:121
  311.5 3.6 collective-permute-start.2
  315.1 1.9 collective-permute-start.3
  317.0 85.9 %psum.23 = f32[192]{0:T(256)} all-reduce(f32[192]{0:T(256)S(1)} %get-tuple-element.148), channel_id=1, replica_groups=mesh['seq'=64,'dp'=4] {'seq','dp'}, use_global_device_ids=true, to_apply=%region_28.29 | all-reduce | flops 192 | bytes 1536 | tf_op jit(solution)/shard_map/psum | solution.py:182
  404.5 9.0 %gather_fusion.7 = bf16[2048,192]{1,0:T(8,128)(2,1)} fusion(bf16[4096,192]{1,0:T(8,128)(2,1)S(1)} %pad_maximum_fusion.6, s32[2048]{0:T(1024)S(1)} %fusion.93), kind=kCustom, calls=%fused_computation.7 | custom fusion | bytes 1581056 | tf_op jit(solution)/shard_map/gather | solution.py:185
  413.5 2.2 copy.28
  417.3 7.5 %gather_fusion.3 = bf16[2048,192]{1,0:T(8,128)(2,1)S(1)} fusion(bf16[4096,192]{1,0:T(8,128)(2,1)S(1)} %pad_maximum_fusion.4, s32[2048]{0:T(1024)S(1)} %fusion.93), kind=kCustom, calls=%fused_computation.3 | custom fusion | bytes 1581056 | tf_op jit(solution)/shard_map/gather | solution.py:121
  426.0 150.5 %all-reduce.3.cloned.1.call-done = (f32[192,576]{1,0:T(8,128)}, f32[192,192]{1,0:T(8,128)}) async-done(((f32[192,576]{1,0:T(8,128)}, f32[192,192]{1,0:T(8,128)}), (f32[192,576]{1,0:T(8,128)}, f32[192,192]{1,0:T(8,128)})) %all-reduce.3.cloned.1.call-update) | async-done | bytes 589840 | tf_op jit(solution)/shard_map/psum | solution.py:182
  576.5 1.8 copy.67
  (176 shorter events, 50.9 us)
Async XLA Ops:
  7.2 569.3 %all-reduce.3.cloned.1.call-start = ((), (), s32[]{:S(2)}) async-start(), calls=%async_computation | async-start | bytes 1376256 | tf_op jit(solution)/shard_map/psum | solution.py:182
  14.4 15.7 %copy-start.19 = (bf16[1,2048,192]{1,2,0:T(8,128)(2,1)S(1)}, bf16[1,2048,192]{1,2,0:T(8,128)(2,1)}, u32[]{:S(2)}) copy-start(bf16[1,2048,192]{1,2,0:T(8,128)(2,1)} %param.13) | copy-start | bytes 2359300
  21.9 8.7 %copy-start.6 = (bf16[2048,192]{1,0:T(8,128)(2,1)}, bf16[2048,192]{1,0:T(8,128)(2,1)S(1)}, u32[]{:S(2)}) copy-start(bf16[2048,192]{1,0:T(8,128)(2,1)S(1)} %gather_fusion) | copy-start | bytes 2359300
  22.9 61.0 %collective-permute-start = (bf16[1024,192]{1,0:T(8,128)(2,1)}, bf16[1024,192]{1,0:T(8,128)(2,1)}, u32[]{:S(2)}, u32[]{:S(2)}) collective-permute-start(bf16[1024,192]{1,0:T(8,128)(2,1)} %get-tuple-element.312), channel_id=1, source_target_pairs={{0,4},{4,8},{8,12},{12,16},{16,20},{20,24},{24,28},{28,32},{32,36}... | collective-permute-start | bytes 1179656 | tf_op jit(solution)/shard_map/ppermute | solution.py:21
  27.8 56.1 %collective-permute-start.1 = (bf16[1024,192]{1,0:T(8,128)(2,1)S(1)}, bf16[1024,192]{1,0:T(8,128)(2,1)}, u32[]{:S(2)}, u32[]{:S(2)}) collective-permute-start(bf16[1024,192]{1,0:T(8,128)(2,1)S(1)} %get-tuple-element.313), channel_id=1, source_target_pairs={{4,0},{8,4},{12,8},{16,12},{20,16},{24,20},{28,24},{32,28},{36,32}... | collective-permute-start | bytes 1179656 | tf_op jit(solution)/shard_map/ppermute | solution.py:22
  30.6 13.9 %copy-start.23 = (s32[1,2048]{1,0:T(1,128)S(1)}, s32[1,2048]{1,0:T(1,128)}, u32[]{:S(2)}) copy-start(s32[1,2048]{1,0:T(1,128)} %param.17) | copy-start | bytes 24580
  30.7 13.9 %copy-start.24 = (s32[1,2048]{1,0:T(1,128)S(1)}, s32[1,2048]{1,0:T(1,128)}, u32[]{:S(2)}) copy-start(s32[1,2048]{1,0:T(1,128)} %param.18) | copy-start | bytes 24580
  38.2 45.7 %copy-start.5 = (bf16[2048,192]{1,0:T(8,128)(2,1)}, bf16[2048,192]{1,0:T(8,128)(2,1)S(1)}, u32[]{:S(2)}) copy-start(bf16[2048,192]{1,0:T(8,128)(2,1)S(1)} %gather_fusion.4) | copy-start | bytes 2359300
  39.3 98.7 %collective-permute-start.4 = (bf16[1024,192]{1,0:T(8,128)(2,1)}, bf16[1024,192]{1,0:T(8,128)(2,1)}, u32[]{:S(2)}, u32[]{:S(2)}) collective-permute-start(bf16[1024,192]{1,0:T(8,128)(2,1)} %get-tuple-element.308), channel_id=1, source_target_pairs={{0,4},{4,8},{8,12},{12,16},{16,20},{20,24},{24,28},{28,32},{32,36}... | collective-permute-start | bytes 1179656 | tf_op jit(solution)/shard_map/ppermute | solution.py:21
  42.6 96.6 %collective-permute-start.5 = (bf16[1024,192]{1,0:T(8,128)(2,1)}, bf16[1024,192]{1,0:T(8,128)(2,1)}, u32[]{:S(2)}, u32[]{:S(2)}) collective-permute-start(bf16[1024,192]{1,0:T(8,128)(2,1)} %get-tuple-element.309), channel_id=1, source_target_pairs={{4,0},{8,4},{12,8},{16,12},{20,16},{24,20},{28,24},{32,28},{36,32}... | collective-permute-start | bytes 1179656 | tf_op jit(solution)/shard_map/ppermute | solution.py:22
  85.8 11.1 %copy-start.21 = (f32[192]{0:T(256)S(1)}, f32[192]{0:T(256)}, u32[]{:S(2)}) copy-start(f32[192]{0:T(256)} %param.14) | copy-start | bytes 2308
  95.6 5.4 copy-start.11
  95.6 5.4 copy-start.18
  95.6 5.4 copy-start.28
  111.4 5.9 %copy-start.15 = (bf16[2,1024,192]{1,2,0:T(8,128)(2,1)S(1)}, bf16[2,1024,192]{1,2,0:T(8,128)(2,1)}, u32[]{:S(2)}) copy-start(bf16[2,1024,192]{1,2,0:T(8,128)(2,1)} %get-tuple-element.519) | copy-start | bytes 2359300 | tf_op jit(solution)/shard_map/while
  129.9 5.9 %copy-start.15 = (bf16[2,1024,192]{1,2,0:T(8,128)(2,1)S(1)}, bf16[2,1024,192]{1,2,0:T(8,128)(2,1)}, u32[]{:S(2)}) copy-start(bf16[2,1024,192]{1,2,0:T(8,128)(2,1)} %get-tuple-element.519) | copy-start | bytes 2359300 | tf_op jit(solution)/shard_map/while
  137.1 0.9 copy-start.16
  138.0 1.0 copy-start.1
  138.0 1.2 copy-start.3
  141.1 11.4 %copy-start.2 = (bf16[2,1024,192]{2,1,0:T(8,128)(2,1)S(1)}, bf16[2,1024,192]{2,1,0:T(8,128)(2,1)}, u32[]{:S(2)}) copy-start(bf16[2,1024,192]{2,1,0:T(8,128)(2,1)} %copy-done.1) | copy-start | bytes 2359300
  141.1 11.4 %copy-start.22 = (f32[192]{0:T(256)S(1)}, f32[192]{0:T(256)}, u32[]{:S(2)}) copy-start(f32[192]{0:T(256)} %param.14) | copy-start | bytes 2308
  152.5 134.1 %copy-start.20 = (s32[2048]{0:T(1024)S(1)}, s32[2048]{0:T(1024)}, u32[]{:S(2)}) copy-start(s32[2048]{0:T(1024)} %fusion.92) | copy-start | bytes 24580
  205.6 6.8 %copy-start.30 = (bf16[3,64,1024]{2,1,0:T(8,128)(2,1)}, bf16[3,64,1024]{2,1,0:T(8,128)(2,1)S(1)}, u32[]{:S(2)}) copy-start(bf16[3,64,1024]{2,1,0:T(8,128)(2,1)S(1)} %fusion.194) | copy-start | bytes 1179652 | tf_op jit(solution)/shard_map/while
  205.6 6.8 %copy-start = (f32[2,1024,192]{1,2,0:T(8,128)S(1)}, f32[2,1024,192]{1,2,0:T(8,128)}, u32[]{:S(2)}) copy-start(f32[2,1024,192]{1,2,0:T(8,128)} %get-tuple-element.583) | copy-start | bytes 4718596 | tf_op jit(solution)/shard_map/while
  205.6 6.8 %copy-start.12 = (bf16[192,576]{1,0:T(8,128)(2,1)S(1)}, bf16[192,576]{1,0:T(8,128)(2,1)}, u32[]{:S(2)}) copy-start(bf16[192,576]{1,0:T(8,128)(2,1)} %get-tuple-element.584) | copy-start | bytes 663556 | tf_op jit(solution)/shard_map/while
  205.6 6.8 %copy-start.29 = (bf16[3,64,1024]{2,1,0:T(8,128)(2,1)S(1)}, bf16[3,64,1024]{2,1,0:T(8,128)(2,1)}, u32[]{:S(2)}) copy-start(bf16[3,64,1024]{2,1,0:T(8,128)(2,1)} %fusion.195) | copy-start | bytes 1179652 | tf_op jit(solution)/shard_map/while
  212.4 1.8 copy-start.31
  212.4 1.5 copy-start.13
  213.1 4.7 copy-start.4
  213.1 4.7 copy-start.9
  271.8 6.8 %copy-start.30 = (bf16[3,64,1024]{2,1,0:T(8,128)(2,1)}, bf16[3,64,1024]{2,1,0:T(8,128)(2,1)S(1)}, u32[]{:S(2)}) copy-start(bf16[3,64,1024]{2,1,0:T(8,128)(2,1)S(1)} %fusion.194) | copy-start | bytes 1179652 | tf_op jit(solution)/shard_map/while
  271.8 6.8 %copy-start = (f32[2,1024,192]{1,2,0:T(8,128)S(1)}, f32[2,1024,192]{1,2,0:T(8,128)}, u32[]{:S(2)}) copy-start(f32[2,1024,192]{1,2,0:T(8,128)} %get-tuple-element.583) | copy-start | bytes 4718596 | tf_op jit(solution)/shard_map/while
  271.8 6.8 %copy-start.12 = (bf16[192,576]{1,0:T(8,128)(2,1)S(1)}, bf16[192,576]{1,0:T(8,128)(2,1)}, u32[]{:S(2)}) copy-start(bf16[192,576]{1,0:T(8,128)(2,1)} %get-tuple-element.584) | copy-start | bytes 663556 | tf_op jit(solution)/shard_map/while
  271.8 6.8 %copy-start.29 = (bf16[3,64,1024]{2,1,0:T(8,128)(2,1)S(1)}, bf16[3,64,1024]{2,1,0:T(8,128)(2,1)}, u32[]{:S(2)}) copy-start(bf16[3,64,1024]{2,1,0:T(8,128)(2,1)} %fusion.195) | copy-start | bytes 1179652 | tf_op jit(solution)/shard_map/while
  278.6 1.8 copy-start.31
  278.6 1.5 copy-start.13
  279.3 4.8 copy-start.4
  279.3 4.8 copy-start.9
  286.6 14.5 %copy-start.25 = (s32[2048]{0:T(1024)S(1)}, s32[2048]{0:T(1024)}, u32[]{:S(2)}) copy-start(s32[2048]{0:T(1024)} %scatter_custom_fusion.1) | copy-start | bytes 24580
  286.6 14.5 %copy-start.26 = (pred[2048]{0:T(1024)(128)(4,1)S(1)}, pred[2048]{0:T(1024)(128)(4,1)}, u32[]{:S(2)}) copy-start(pred[2048]{0:T(1024)(128)(4,1)} %get-tuple-element.280) | copy-start | bytes 6148
  286.6 14.5 %copy-start.27 = (pred[2048]{0:T(1024)(128)(4,1)S(1)}, pred[2048]{0:T(1024)(128)(4,1)}, u32[]{:S(2)}) copy-start(pred[2048]{0:T(1024)(128)(4,1)} %get-tuple-element.283) | copy-start | bytes 6148
  286.6 15.6 %copy-start.17 = (bf16[2,1024,192]{1,2,0:T(8,128)(2,1)S(1)}, bf16[2,1024,192]{1,2,0:T(8,128)(2,1)}, u32[]{:S(2)}) copy-start(bf16[2,1024,192]{1,2,0:T(8,128)(2,1)} %get-tuple-element.140) | copy-start | bytes 2359300
  295.5 107.4 %collective-permute-start.6 = (bf16[1024,192]{1,0:T(8,128)(2,1)}, bf16[1024,192]{1,0:T(8,128)(2,1)}, u32[]{:S(2)}, u32[]{:S(2)}) collective-permute-start(bf16[1024,192]{1,0:T(8,128)(2,1)} %get-tuple-element.306), channel_id=1, source_target_pairs={{0,4},{4,8},{8,12},{12,16},{16,20},{20,24},{24,28},{28,32},{32,36}... | collective-permute-start | bytes 1179656 | tf_op jit(solution)/shard_map/ppermute | solution.py:21
  299.2 103.8 %collective-permute-start.7 = (bf16[1024,192]{1,0:T(8,128)(2,1)}, bf16[1024,192]{1,0:T(8,128)(2,1)}, u32[]{:S(2)}, u32[]{:S(2)}) collective-permute-start(bf16[1024,192]{1,0:T(8,128)(2,1)} %get-tuple-element.307), channel_id=1, source_target_pairs={{4,0},{8,4},{12,8},{16,12},{20,16},{24,20},{28,24},{32,28},{36,32}... | collective-permute-start | bytes 1179656 | tf_op jit(solution)/shard_map/ppermute | solution.py:22
  310.3 92.6 %copy-start.7 = (bf16[2048,192]{1,0:T(8,128)(2,1)}, bf16[2048,192]{1,0:T(8,128)(2,1)S(1)}, u32[]{:S(2)}) copy-start(bf16[2048,192]{1,0:T(8,128)(2,1)S(1)} %gather_fusion.2) | copy-start | bytes 2359300
  311.5 104.3 %collective-permute-start.2 = (bf16[1024,192]{1,0:T(8,128)(2,1)}, bf16[1024,192]{1,0:T(8,128)(2,1)}, u32[]{:S(2)}, u32[]{:S(2)}) collective-permute-start(bf16[1024,192]{1,0:T(8,128)(2,1)} %get-tuple-element.310), channel_id=1, source_target_pairs={{0,4},{4,8},{8,12},{12,16},{16,20},{20,24},{24,28},{28,32},{32,36}... | collective-permute-start | bytes 1179656 | tf_op jit(solution)/shard_map/ppermute | solution.py:21
  315.1 100.6 %collective-permute-start.3 = (bf16[1024,192]{1,0:T(8,128)(2,1)}, bf16[1024,192]{1,0:T(8,128)(2,1)}, u32[]{:S(2)}, u32[]{:S(2)}) collective-permute-start(bf16[1024,192]{1,0:T(8,128)(2,1)} %get-tuple-element.311), channel_id=1, source_target_pairs={{4,0},{8,4},{12,8},{16,12},{20,16},{24,20},{28,24},{32,28},{36,32}... | collective-permute-start | bytes 1179656 | tf_op jit(solution)/shard_map/ppermute | solution.py:22
  404.5 11.2 %copy-start.8 = (bf16[2048,192]{1,0:T(8,128)(2,1)S(1)}, bf16[2048,192]{1,0:T(8,128)(2,1)}, u32[]{:S(2)}) copy-start(bf16[2048,192]{1,0:T(8,128)(2,1)} %copy-done.7) | copy-start | bytes 2359300
  (5 other events, 4.0 us)
Sparse Core Ops, SparseCore 0:
  317.2 259.2 all-reduce.2
where the time goes:
time: 588 us; the launch traced here: 587 us
  matrix products  154 us (26%)
  waiting for transfers between devices  151 us (26%)
  local copies, waits for them, and re-layouts  114 us (19%)
  blocking collectives  85.9 us (15%)
  other arithmetic  41 us (7%)
  starting transfers between devices  23.5 us (4%)
  between operations  17 us (3%)
    psum x1, waiting for transfers between devices, shards(): lax.psum((local_totals[0], local_totals[1], local_totals[2]), ('seq', 'dp'))  150 us
    psum x1, blocking collectives, shards(): lax.psum((local_totals[0], local_totals[1], local_totals[2]), ('seq', 'dp'))  85.9 us
    dot_general x2, matrix products, patch_backward(): jnp.einsum('hqk,khd->qhd', d_scores, keys_h, preferred_element_type=jnp.f...  36.8 us
    dot_general x2, matrix products, patch_backward(): jnp.einsum('hqk,qhd->khd', d_scores, queries, preferred_element_type=jnp....  35.7 us
    sub x4, matrix products, probabilities(): weights = jnp.exp(scores - highest)  30.1 us
    gather x2, local copies, waits for them, and re-layouts, shards(): dx_zor = extended(dx_hil[send_back], (('seq', 0),), spill)[place_back]  16.8 us
    scatter x2, local copies, waits for them, and re-layouts, route_plan(): jnp.zeros((per_dev,), jnp.int32).at[group_order]  16.7 us
    gather x2, local copies, waits for them, and re-layouts, shards(): g_hil = extended(grad_out[0][send_fwd], (('seq', 0),), spill)[place_fwd]  16.5 us
  transfers between devices with their start and end apart: 9, of which 1 were waited for; matrix products, arithmetic and copies ran while one was open for 22% of the time, Pallas kernels for 0%

commit v1 on v0

v1 whole, which is shorter than its diff:
```python
import functools

import jax
import jax.numpy as jnp
from jax import lax
from jax.experimental import pallas as pl
from jax.experimental.pallas import tpu as pltpu
from jax.sharding import PartitionSpec as P

HEADS = 3
PATCH = 1024
C = 192
D = 64
HP = 128
N = 2048
EPS = 1e-5
LOG2E = 1.4426950408889634
BF = jnp.bfloat16
F32 = jnp.float32
MESH = pl.DeviceIdType.MESH
VMEM_LIMIT = 60 * 2**20
GROUP = 16
TILES = 10


def dot(a, b):
    return jnp.dot(a, b, preferred_element_type=F32)


def dot_nt(a, b):
    return lax.dot_general(a, b, (((1,), (1,)), ((), ())), preferred_element_type=F32)


def dot_tn(a, b):
    return lax.dot_general(a, b, (((0,), (0,)), ((), ())), preferred_element_type=F32)


def gather_kernel(idx_ref, *refs):
    ins, outs, (src, dst) = refs[:6], refs[6:8], refs[8:]
    for i in range(3):
        for a in range(2):
            ref = ins[3 * a + i]

            def fill(t, c, ref=ref, i=i, a=a):
                rows = ref[pl.ds(t * 256, 256), :].astype(F32)
                at = i * 4 * N + t * 1024 + 2 * a
                src[pl.ds(at, 256, stride=4), :] = rows[:, :HP]
                tail = jnp.concatenate([rows[:, HP:], jnp.zeros((256, D), F32)], axis=1)
                src[pl.ds(at + 1, 256, stride=4), :] = tail
                return c

            lax.fori_loop(0, N // 256, fill, 0)

    def body(t, c):
        for u in range(16):
            j = t * 16 + u
            dst[pl.ds(pl.multiple_of(4 * j, 4), 4), :] = src[
                pl.ds(pl.multiple_of(idx_ref[j], 4), 4), :
            ]
        return c

    lax.fori_loop(0, N // 16, body, 0)

    for a in range(2):

        def out(t, c, a=a):
            at = t * 1024 + 2 * a
            head = dst[pl.ds(at, 256, stride=4), :]
            tail = dst[pl.ds(at + 1, 256, stride=4), :]
            outs[a][pl.ds(t * 256, 256), :] = jnp.concatenate([head, tail[:, :D]], axis=1).astype(BF)
            return c

        lax.fori_loop(0, N // 256, out, 0)


def gather(idx4, first, second):
    row = jax.ShapeDtypeStruct((N, C), BF)
    return pl.pallas_call(
        gather_kernel,
        out_shape=(row, row),
        in_specs=[pl.BlockSpec(memory_space=pltpu.SMEM)]
        + [pl.BlockSpec(memory_space=pltpu.VMEM)] * 6,
        scratch_shapes=[pltpu.VMEM((12 * N, HP), F32), pltpu.VMEM((4 * N, HP), F32)],
        compiler_params=pltpu.CompilerParams(vmem_limit_bytes=VMEM_LIMIT),
        name="rows",
    )(idx4, *first, *second)


def attn_kernel(
    QB,
    cnt_ref, x_ref, g_ref, gain_ref, wqkv_ref, wqkvT_ref, wproj_ref, wprojT_ref,
    y_ref, dx_ref, tot_ref,
    normed, qkv, dattn, attn, dqkv, dkacc, dvacc, gqkv, gproj, ggain,
):
    p = pl.program_id(0)
    live_n = cnt_ref[p]
    gain = gain_ref[...]
    x = x_ref[...].astype(F32)
    center = x - jnp.mean(x, axis=-1, keepdims=True)
    inv = lax.rsqrt(jnp.mean(center * center, axis=-1, keepdims=True) + EPS)
    unit = center * inv
    normed[...] = (unit * gain).astype(BF)
    row = lax.broadcasted_iota(jnp.int32, (PATCH, HP), 0)
    lane = lax.broadcasted_iota(jnp.int32, (PATCH, HP), 1)
    live = row[:, :1] < live_n
    livef = live.astype(F32)
    gl = jnp.where(live, g_ref[...].astype(F32), 0.0).astype(BF)
    nm = normed[...]
    bias = jnp.where(row < live_n, 0.0, -1e30)
    for h in range(HEADS):
        q = dot(nm, wqkv_ref[:, h * HP : (h + 1) * HP])
        q = q.astype(BF).astype(F32) * 0.125
        qkv[:, h * HP : (h + 1) * HP] = jnp.where(lane == D, 1.0, q).astype(BF)
        k = dot(nm, wqkv_ref[:, (3 + h) * HP : (4 + h) * HP])
        qkv[:, (3 + h) * HP : (4 + h) * HP] = jnp.where(lane == D, bias, k).astype(BF)
        v = dot(nm, wqkv_ref[:, (6 + h) * HP : (7 + h) * HP])
        qkv[:, (6 + h) * HP : (7 + h) * HP] = v.astype(BF)
        dattn[:, h * HP : (h + 1) * HP] = dot(gl, wprojT_ref[:, h * HP : (h + 1) * HP]).astype(BF)
    for h in range(HEADS):
        qq = slice(h * HP, (h + 1) * HP)
        kk = slice((3 + h) * HP, (4 + h) * HP)
        vv = slice((6 + h) * HP, (7 + h) * HP)
        k = qkv[:, kk]
        v = qkv[:, vv]
        for b in range(PATCH // QB):
            rs = slice(b * QB, (b + 1) * QB)
            qb = qkv[rs, qq]
            dob = dattn[rs, qq]
            s = dot_nt(qb, k)
            m = jnp.max(s, axis=-1, keepdims=True)
            e = jnp.exp2((s - m) * LOG2E)
            l = jnp.sum(e, axis=-1, keepdims=True)
            pn = e * (1.0 / l)
            pb = pn.astype(BF)
            o = dot(pb, v)
            attn[rs, qq] = o.astype(BF)
            dp = dot_nt(dob, v)
            delta = jnp.sum(o * dob.astype(F32), axis=-1, keepdims=True)
            ds = (pn * (dp - delta)).astype(BF)
            dqkv[rs, qq] = (dot(ds, k) * 0.125).astype(BF)
            dk = dot_tn(qb, ds)
            dv = dot_tn(dob, pb)
            if b == 0:
                dkacc[...] = dk
                dvacc[...] = dv
            else:
                dkacc[...] += dk
                dvacc[...] += dv
        dqkv[:, kk] = dkacc[...].T.astype(BF)
        dqkv[:, vv] = dvacc[...].T.astype(BF)
    at = attn[...]
    branch = dot(at, wproj_ref[...])
    y_ref[...] = (x + livef * branch).astype(BF)
    gp = dot_tn(at, gl)
    dq = dqkv[...]
    gq = dot_tn(nm, dq)
    dn = dot(dq, wqkvT_ref[...])
    gg = jnp.sum(unit * dn, axis=0, keepdims=True)
    du = dn * gain
    dr = inv * (
        du
        - jnp.mean(du, axis=-1, keepdims=True)
        - unit * jnp.mean(du * unit, axis=-1, keepdims=True)
    )
    dx_ref[...] = (g_ref[...].astype(F32) + dr).astype(BF)

    @pl.when(p == 0)
    def _():
        gqkv[...] = gq
        gproj[...] = gp
        ggain[...] = gg

    @pl.when(p != 0)
    def _():
        def half(i):
            return (gqkv[:, i * HP : i * HP + D] + gq[:, i * HP : i * HP + D]) if i < 9 else (
                jnp.concatenate(
                    [
                        gproj[h * HP : h * HP + D, (i - 9) * D : (i - 8) * D]
                        + gp[h * HP : h * HP + D, (i - 9) * D : (i - 8) * D]
                        for h in range(HEADS)
                    ],
                    axis=0,
                )
            )

        for ct in range(6):
            cols = jnp.concatenate([half(2 * ct), half(2 * ct + 1)], axis=1)
            for rt in range(24):
                t = rt * 6 + ct
                tot_ref[t // 9, t % 9, :, :] = cols[rt * 8 : (rt + 1) * 8, :]
        tot_ref[:, 9, :, :] = jnp.zeros((GROUP, 8, HP), F32)
        whole = ggain[...] + gg
        tot_ref[0, 9, 0:1, :] = whole[:, :HP]
        tot_ref[0, 9, 1:2, :D] = whole[:, HP:]


def pad_heads(w, n, axis):
    w = jnp.moveaxis(w, axis, -1)
    s = w.shape
    w = w.reshape(s[:-1] + (n, D))
    w = jnp.pad(w, [(0, 0)] * len(s[:-1]) + [(0, 0), (0, HP - D)])
    return jnp.moveaxis(w.reshape(s[:-1] + (n * HP,)), -1, axis)


def attn_call(cnt, x, g, gain, wqkv, wproj, QB=512):
    wq = pad_heads(wqkv, 9, 1)
    wp = pad_heads(wproj, 3, 0)

    def full(shape):
        return pl.BlockSpec(shape, lambda p: (0,) * len(shape))

    rows = pl.BlockSpec((PATCH, C), lambda p: (p, 0))
    return pl.pallas_call(
        functools.partial(attn_kernel, QB),
        grid=(2,),
        out_shape=(
            jax.ShapeDtypeStruct((N, C), BF),
            jax.ShapeDtypeStruct((N, C), BF),
            jax.ShapeDtypeStruct((GROUP, TILES, 8, HP), F32),
        ),
        in_specs=[
            pl.BlockSpec(memory_space=pltpu.SMEM),
            rows, rows,
            full((1, C)), full((C, 9 * HP)), full((9 * HP, C)), full((3 * HP, C)), full((C, 3 * HP)),
        ],
        out_specs=(rows, rows, full((GROUP, TILES, 8, HP))),
        scratch_shapes=[
            pltpu.VMEM((PATCH, C), BF), pltpu.VMEM((PATCH, 9 * HP), BF), pltpu.VMEM((PATCH, 3 * HP), BF),
            pltpu.VMEM((PATCH, 3 * HP), BF), pltpu.VMEM((PATCH, 9 * HP), BF),
            pltpu.VMEM((HP, PATCH), F32), pltpu.VMEM((HP, PATCH), F32),
            pltpu.VMEM((C, 9 * HP), F32), pltpu.VMEM((3 * HP, C), F32), pltpu.VMEM((1, C), F32),
        ],
        compiler_params=pltpu.CompilerParams(vmem_limit_bytes=VMEM_LIMIT),
        name="attention",
    )(cnt, x, g, gain.reshape(1, C), wq, wq.T, wp, wp.T)


def reduce_kernel(
    tot_ref, gqkv_ref, gproj_ref, ggain_ref,
    recv_a, sum_a, recv_b, fin, out_b, out_a,
    sa, ra, sb, rb, sc, rc, sd, rd,
):
    seq = lax.axis_index("seq")
    x = lax.axis_index("dp")
    y = seq // GROUP
    b = seq % GROUP
    a = y * 4 + x

    def dev_a(i):
        o = (a + i) % GROUP
        return o, {"dp": o % 4, "seq": (o // 4) * GROUP + b}

    def dev_b(i):
        o = (b + i) % GROUP
        return o, {"dp": x, "seq": y * GROUP + o}

    barrier = pltpu.get_barrier_semaphore()

    def greet(i, c):
        pl.semaphore_signal(barrier, inc=1, device_id=dev_a(i)[1], device_id_type=MESH)
        pl.semaphore_signal(barrier, inc=1, device_id=dev_b(i)[1], device_id_type=MESH)
        return c

    lax.fori_loop(1, GROUP, greet, 0)
    pl.semaphore_wait(barrier, 2 * (GROUP - 1))

    def loop(f, lo=1, hi=GROUP):
        def body(i, c):
            f(i)
            return c

        lax.fori_loop(lo, hi, body, 0)

    def copy_a(i):
        o, dev = dev_a(i)
        return pltpu.make_async_remote_copy(
            tot_ref.at[o], recv_a.at[a], sa.at[o], ra.at[a], device_id=dev, device_id_type=MESH
        )

    def into_a(o):
        return pltpu.make_async_remote_copy(
            tot_ref.at[o], recv_a.at[o], sa.at[o], ra.at[o],
            device_id=dev_a(1)[1], device_id_type=MESH,
        )

    recv_a[a] = tot_ref[a]
    loop(lambda i: copy_a(i).start())
    loop(lambda i: into_a((a + GROUP - i) % GROUP).wait_recv())
    acc = recv_a[0]
    for i in range(1, GROUP):
        acc = acc + recv_a[i]
    sum_a[...] = acc

    def copy_b(t):
        return pltpu.make_async_remote_copy(
            sum_a.at[t], recv_b.at[b], sb.at[t], rb.at[b],
            device_id={"dp": x, "seq": y * GROUP + t}, device_id_type=MESH,
        )

    def into_b(o):
        return pltpu.make_async_remote_copy(
            sum_a.at[0], recv_b.at[o], sb.at[0], rb.at[o],
            device_id=dev_b(1)[1], device_id_type=MESH,
        )

    def send_b(t):
        @pl.when(t != b)
        def _():
            copy_b(t).start()

    loop(send_b, 0, TILES)

    def copy_c(i):
        o, dev = dev_b(i)
        return pltpu.make_async_remote_copy(
            out_b.at[b], out_b.at[b], sc.at[o], rc.at[b], device_id=dev, device_id_type=MESH
        )

    def into_c(o):
        return pltpu.make_async_remote_copy(
            out_b.at[o], out_b.at[o], sc.at[o], rc.at[o],
            device_id=dev_b(1)[1], device_id_type=MESH,
        )

    @pl.when(b < TILES)
    def _():
        recv_b[b] = sum_a[b]
        loop(lambda i: into_b((b + GROUP - i) % GROUP).wait_recv())
        total = recv_b[0]
        for i in range(1, GROUP):
            total = total + recv_b[i]
        out_b[b] = total
        loop(lambda i: copy_c(i).start())

    def wait_c(t):
        @pl.when(t != b)
        def _():
            into_c(t).wait_recv()

    loop(wait_c, 0, TILES)

    def copy_d(i):
        o, dev = dev_a(i)
        return pltpu.make_async_remote_copy(
            out_b, out_a.at[a], sd.at[o], rd.at[a], device_id=dev, device_id_type=MESH
        )

    def into_d(o):
        return pltpu.make_async_remote_copy(
            out_b, out_a.at[o], sd.at[o], rd.at[o],
            device_id=dev_a(1)[1], device_id_type=MESH,
        )

    loop(lambda i: copy_d(i).start())
    out_a[a] = out_b[...]
    loop(lambda i: into_d((a + GROUP - i) % GROUP).wait_recv())

    def tile(rt, ct):
        t = rt * 6 + ct
        return out_a[t // 9, t % 9, :, :]

    for rt in range(24):
        rows = slice(rt * 8, (rt + 1) * 8)
        for ct in range(4):
            gqkv_ref[rows, ct * HP : (ct + 1) * HP] = tile(rt, ct)
        mid = tile(rt, 4)
        gqkv_ref[rows, 4 * HP :] = mid[:, :D]
        gproj_ref[rows, :] = jnp.concatenate([mid[:, D:], tile(rt, 5)], axis=1)
    ggain_ref[:, :HP] = out_a[0, 9, 0:1, :]
    ggain_ref[:, HP:] = out_a[0, 9, 1:2, :D]

    loop(lambda i: copy_a(i).wait_send())

    def sent_b(t):
        @pl.when(t != b)
        def _():
            copy_b(t).wait_send()

    loop(sent_b, 0, TILES)

    @pl.when(b < TILES)
    def _():
        loop(lambda i: copy_c(i).wait_send())

    loop(lambda i: copy_d(i).wait_send())


def reduce_all(tot):
    vmem = pl.BlockSpec(memory_space=pltpu.VMEM)
    return pl.pallas_call(
        reduce_kernel,
        out_shape=(
            jax.ShapeDtypeStruct((C, 3 * C), F32),
            jax.ShapeDtypeStruct((C, C), F32),
            jax.ShapeDtypeStruct((1, C), F32),
        ),
        in_specs=[vmem],
        out_specs=(vmem, vmem, vmem),
        scratch_shapes=[
            pltpu.VMEM((GROUP, TILES, 8, HP), F32),
            pltpu.VMEM((TILES, 8, HP), F32),
            pltpu.VMEM((GROUP, 8, HP), F32),
            pltpu.VMEM((8, HP), F32),
            pltpu.VMEM((TILES, 8, HP), F32),
            pltpu.VMEM((GROUP, TILES, 8, HP), F32),
        ]
        + [pltpu.SemaphoreType.DMA((GROUP,))] * 8,
        compiler_params=pltpu.CompilerParams(
            collective_id=0, has_side_effects=True, vmem_limit_bytes=VMEM_LIMIT
        ),
        name="reduce",
    )(tot)


def sides(v):
    peers = lax.axis_size("seq")
    up = [(i, i + 1) for i in range(peers - 1)]
    down = [(j, i) for i, j in up]
    return lax.ppermute(v, "seq", up), v, lax.ppermute(v, "seq", down)


def shards(features, grad_out, norm_gain, w_qkv, w_proj, to_hilbert, to_zorder, counts):
    base = (lax.axis_index("seq") - 1) * N
    x_hil, g_hil = gather((to_zorder[0] - base) * 4, sides(features[0]), sides(grad_out[0]))
    y_hil, dx_hil, tot = attn_call(counts[0], x_hil, g_hil, norm_gain, w_qkv, w_proj)
    grad_qkv, grad_proj, grad_gain = reduce_all(tot)
    y_zor, dx_zor = gather((to_hilbert[0] - base) * 4, sides(y_hil), sides(dx_hil))
    return (y_zor[None], dx_zor[None], grad_qkv, grad_proj, grad_gain[0])


def solution(mesh):
    rows = P("dp", "seq", None)
    in_specs = (rows, rows, P(), P(), P(), P("dp", "seq"), P("dp", "seq"), P("dp", "seq"))
    out_specs = (rows, rows, P(), P(), P())
    return jax.shard_map(shards, mesh=mesh, in_specs=in_specs, out_specs=out_specs, check_vma=False)
```

time: 588 us -> 159 us (0.27)
  matrix products: 154 us -> 0 us
  waiting for transfers between devices: 151 us -> 2.07 us
  Pallas kernels: 0 us -> 103 us
  local copies, waits for them, and re-layouts: 114 us -> 27.9 us
  blocking collectives: 85.9 us -> 0 us
  other arithmetic: 41 us -> 1.22 us
  between operations: 17 us -> 0.87 us
    psum x1 -> x0, waiting for transfers between devices: 150 us -> none  [shards(): lax.psum((local_totals[0], local_totals[1], local_totals[2]), ('seq', 'dp'))]
    dot_general x22 -> x0, matrix products: 124 us -> none  [the longest x2 36.8 us: patch_backward(): jnp.einsum('hqk,khd->qhd', d_scores, keys_h, preferred_element_type=jnp.f...]
    pallas_call x0 -> x4, Pallas kernels: none -> 103 us  [the longest x1 49.3 us: reduce_all(): pl.pallas_call(reduce_kernel, out_shape=(jax.ShapeDtypeStruct((C, 3 * C),...]
    psum x1 -> x0, blocking collectives: 85.9 us -> none  [shards(): lax.psum((local_totals[0], local_totals[1], local_totals[2]), ('seq', 'dp'))]
    gather x8 -> x0, local copies, waits for them, and re-layouts: 63.2 us -> none  [the longest x2 16.8 us: shards(): dx_zor = extended(dx_hil[send_back], (('seq', 0),), spill)[place_back]]
    sub x4 -> x0, matrix products: 30.1 us -> none  [probabilities(): weights = jnp.exp(scores - highest)]
    sort x4 -> x0, other arithmetic: 20.9 us -> none  [the longest x2 10.8 us: route_plan(): send_order = jnp.argsort(send_key, stable=True)]
    scatter x2 -> x0, local copies, waits for them, and re-layouts: 16.7 us -> none  [route_plan(): jnp.zeros((per_dev,), jnp.int32).at[group_order]]
  transfers between devices with their start and end apart: 9 -> 8, of which waited for: 1 -> 1; matrix products, arithmetic and copies ran while one was open for 22% -> 12% of each run, Pallas kernels for 0% -> 31%
where the time goes in v1:
time: 159 us; the launch traced here: 158 us
  Pallas kernels  103 us (65%)
  local copies, waits for them, and re-layouts  27.9 us (18%)
  starting transfers between devices  22.8 us (14%)
  waiting for transfers between devices  2.07 us (1%)
    pallas_call x1, Pallas kernels, reduce_all(): pl.pallas_call(reduce_kernel, out_shape=(jax.ShapeDtypeStruct((C, 3 * C),...  49.3 us
    pallas_call x1, Pallas kernels, attn_call(): pl.pallas_call(functools.partial(attn_kernel, QB), grid=(2,), out_shape=(...  37.6 us
    ppermute x8, starting transfers between devices, sides(): return (lax.ppermute(v, 'seq', up), v, lax.ppermute(v, 'seq', down))  22.8 us
    pallas_call x2, Pallas kernels, gather(): pl.pallas_call(gather_kernel, out_shape=(row, row), in_specs=[pl.BlockSpe...  16.5 us
    ppermute x8, local copies, waits for them, and re-layouts, sides(): return (lax.ppermute(v, 'seq', up), v, lax.ppermute(v, 'seq', down))  14.1 us
    unnamed x33, local copies, waits for them, and re-layouts  9.67 us
  transfers between devices with their start and end apart: 8, of which 1 were waited for; matrix products, arithmetic and copies ran while one was open for 12% of the time, Pallas kernels for 31%

profile of v1, /device:TPU:1, one launch (start us, length us, event | category | flops | bytes accessed | tf_op | source)
XLA Modules:
  0.0 158.3 jit_solution(13436334190140698678)
XLA Ops:
  0.6 4.9 %collective-permute-start = (bf16[2048,192]{0,1:T(8,128)(2,1)}, bf16[2048,192]{0,1:T(8,128)(2,1)}, u32[]{:S(2)}, u32[]{:S(2)}) collective-permute-start(bf16[2048,192]{0,1:T(8,128)(2,1)} %bitcast.32), channel_id=1, source_target_pairs={{0,4},{4,8},{8,12},{12,16},{16,20},{20,24},{24,28},{28,32},{32,36}... | collective-permute-start | bytes 2359304 | tf_op jit(solution)/shard_map/ppermute | solution.py:420
  5.6 2.4 %collective-permute-start.1 = (bf16[2048,192]{0,1:T(8,128)(2,1)}, bf16[2048,192]{0,1:T(8,128)(2,1)}, u32[]{:S(2)}, u32[]{:S(2)}) collective-permute-start(bf16[2048,192]{0,1:T(8,128)(2,1)} %bitcast.33), channel_id=1, source_target_pairs={{4,0},{8,4},{12,8},{16,12},{20,16},{24,20},{28,24},{32,28},{36,32}... | collective-permute-start | bytes 2359304 | tf_op jit(solution)/shard_map/ppermute | solution.py:420
  8.0 3.2 %collective-permute-start.2 = (bf16[2048,192]{0,1:T(8,128)(2,1)}, bf16[2048,192]{0,1:T(8,128)(2,1)S(1)}, u32[]{:S(2)}, u32[]{:S(2)}) collective-permute-start(bf16[2048,192]{0,1:T(8,128)(2,1)} %bitcast.34), channel_id=1, source_target_pairs={{0,4},{4,8},{8,12},{12,16},{16,20},{20,24},{24,28},{28,32},{32,36}... | collective-permute-start | bytes 2359304 | tf_op jit(solution)/shard_map/ppermute | solution.py:420
  11.2 1.9 %collective-permute-start.3 = (bf16[2048,192]{0,1:T(8,128)(2,1)}, bf16[2048,192]{0,1:T(8,128)(2,1)S(1)}, u32[]{:S(2)}, u32[]{:S(2)}) collective-permute-start(bf16[2048,192]{0,1:T(8,128)(2,1)} %bitcast.35), channel_id=1, source_target_pairs={{4,0},{8,4},{12,8},{16,12},{20,16},{24,20},{28,24},{32,28},{36,32}... | collective-permute-start | bytes 2359304 | tf_op jit(solution)/shard_map/ppermute | solution.py:420
  13.1 2.3 %copy.29 = bf16[1,2048,192]{2,1,0:T(8,128)(2,1)} copy(bf16[1,2048,192]{1,2,0:T(8,128)(2,1)} %param.8) | data formatting | bytes 1572864 | tf_op args[0]
  15.4 1.3 copy.32
  16.7 0.2 copy.39
  16.9 0.1 pad.8
  16.9 0.0 copy-start
  16.9 0.0 copy-start.8
  17.0 1.0 copy.42.wqkv_ref
  17.9 0.2 copy.40
  18.1 0.1 pad.9
  18.3 0.0 copy-start.9
  18.3 0.8 copy.41
  19.1 0.6 subtract_multiply_fusion
  19.7 0.0 collective-permute-done
  19.7 2.2 %copy.35.refs_0_ = bf16[2048,192]{1,0:T(8,128)(2,1)} copy(bf16[2048,192]{0,1:T(8,128)(2,1)} %collective-permute-done) | data formatting | bytes 1572864 | tf_op jit(solution)/shard_map/ppermute | solution.py:420
  21.9 0.0 collective-permute-done.1
  21.9 2.2 %copy.36.refs_2_ = bf16[2048,192]{1,0:T(8,128)(2,1)} copy(bf16[2048,192]{0,1:T(8,128)(2,1)} %collective-permute-done.1) | data formatting | bytes 1572864 | tf_op jit(solution)/shard_map/ppermute | solution.py:420
  24.2 0.0 collective-permute-done.2
  24.2 1.3 copy.37.refs_3_
  25.5 2.0 %collective-permute-done.3 = bf16[2048,192]{0,1:T(8,128)(2,1)S(1)} collective-permute-done((bf16[2048,192]{0,1:T(8,128)(2,1)}, bf16[2048,192]{0,1:T(8,128)(2,1)S(1)}, u32[]{:S(2)}, u32[]{:S(2)}) %collective-permute-start.3) | collective-permute-done | bytes 786464 | tf_op jit(solution)/shard_map/ppermute | solution.py:420
  27.5 1.3 copy.38.refs_5_
  28.9 8.2 %rows.2 = (bf16[2048,192]{1,0:T(8,128)(2,1)}, bf16[2048,192]{1,0:T(8,128)(2,1)}) custom-call(s32[2048]{0:T(1024)} %bitcast.40, bf16[2048,192]{1,0:T(8,128)(2,1)} %copy.35.refs_0_, bf16[2048,192]{1,0:T(8,128)(2,1)} %bitcast.25, bf16[2048,192]{1,0:T(8,128)(2,1)} %copy.36.refs_2_, bf16[2048,192]{1,0:T(8,128)(2,1)} %copy.37.refs_3_, bf16[2048,192]{1,0:T(8,128)(2,1)} %bitcast.26, ...), custom_call_target="tpu_custom_call" | custom-call | tf_op jit(solution)/shard_map/rows/pallas_call | solution.py:78
  37.1 37.6 %attention.1 = (bf16[2048,192]{1,0:T(8,128)(2,1)}, bf16[2048,192]{1,0:T(8,128)(2,1)}, f32[16,10,8,128]{3,2,1,0:T(8,128)}) custom-call(s32[2]{0:T(128)} %bitcast.43, bf16[2048,192]{1,0:T(8,128)(2,1)} %get-tuple-element.15.x_ref, bf16[2048,192]{1,0:T(8,128)(2,1)} %get-tuple-element.16.g_ref, f32[1,192]{1,0:T(1,128)} %bitcast.41, ...), custom_call_target="tpu_custom_call" | custom-call | tf_op jit(solution)/shard_map/attention/pallas_call | solution.py:214
  74.7 1.5 copy.43
  76.3 1.9 %collective-permute-start.4 = (bf16[2048,192]{0,1:T(8,128)(2,1)S(1)}, bf16[2048,192]{0,1:T(8,128)(2,1)}, u32[]{:S(2)}, u32[]{:S(2)}) collective-permute-start(bf16[2048,192]{0,1:T(8,128)(2,1)S(1)} %copy.43), channel_id=1, source_target_pairs={{0,4},{4,8},{8,12},{12,16},{16,20},{20,24},{24,28},{28,32},{32,36}... | collective-permute-start | bytes 2359304 | tf_op jit(solution)/shard_map/ppermute | solution.py:420
  78.2 3.3 %collective-permute-start.5 = (bf16[2048,192]{0,1:T(8,128)(2,1)S(1)}, bf16[2048,192]{0,1:T(8,128)(2,1)S(1)}, u32[]{:S(2)}, u32[]{:S(2)}) collective-permute-start(bf16[2048,192]{0,1:T(8,128)(2,1)S(1)} %copy.43), channel_id=1, source_target_pairs={{4,0},{8,4},{12,8},{16,12},{20,16},{24,20},{28,24},{32,28},{36,32}... | collective-permute-start | bytes 2359304 | tf_op jit(solution)/shard_map/ppermute | solution.py:420
  81.5 0.0 copy-start.10
  81.5 0.5 copy.45
  82.0 2.6 %collective-permute-start.6 = (bf16[2048,192]{0,1:T(8,128)(2,1)S(1)}, bf16[2048,192]{0,1:T(8,128)(2,1)}, u32[]{:S(2)}, u32[]{:S(2)}) collective-permute-start(bf16[2048,192]{0,1:T(8,128)(2,1)S(1)} %copy.45), channel_id=1, source_target_pairs={{0,4},{4,8},{8,12},{12,16},{16,20},{20,24},{24,28},{28,32},{32,36}... | collective-permute-start | bytes 2359304 | tf_op jit(solution)/shard_map/ppermute | solution.py:420
  84.6 2.6 %collective-permute-start.7 = (bf16[2048,192]{0,1:T(8,128)(2,1)S(1)}, bf16[2048,192]{0,1:T(8,128)(2,1)S(1)}, u32[]{:S(2)}, u32[]{:S(2)}) collective-permute-start(bf16[2048,192]{0,1:T(8,128)(2,1)S(1)} %copy.45), channel_id=1, source_target_pairs={{4,0},{8,4},{12,8},{16,12},{20,16},{24,20},{28,24},{32,28},{36,32}... | collective-permute-start | bytes 2359304 | tf_op jit(solution)/shard_map/ppermute | solution.py:420
  87.3 0.6 subtract_multiply_fusion.1
  87.9 49.3 %reduce.1 = (f32[192,576]{1,0:T(8,128)}, f32[192,192]{1,0:T(8,128)}, f32[1,192]{1,0:T(1,128)}) custom-call(f32[16,10,8,128]{3,2,1,0:T(8,128)} %get-tuple-element.21.tot_ref), custom_call_target="tpu_custom_call" | custom-call | tf_op jit(solution)/shard_map/reduce/pallas_call | solution.py:391
  137.1 0.0 collective-permute-done.4
  137.1 2.2 %copy.47.refs_0_ = bf16[2048,192]{1,0:T(8,128)(2,1)} copy(bf16[2048,192]{0,1:T(8,128)(2,1)} %collective-permute-done.4) | data formatting | bytes 1572864 | tf_op jit(solution)/shard_map/ppermute | solution.py:420
  139.4 1.3 copy.48.refs_2_
  140.6 0.0 collective-permute-done.6
  140.6 2.2 %copy.49.refs_3_ = bf16[2048,192]{1,0:T(8,128)(2,1)} copy(bf16[2048,192]{0,1:T(8,128)(2,1)} %collective-permute-done.6) | data formatting | bytes 1572864 | tf_op jit(solution)/shard_map/ppermute | solution.py:420
  142.9 1.3 copy.50.refs_5_
  144.2 8.3 %rows.3 = (bf16[2048,192]{1,0:T(8,128)(2,1)}, bf16[2048,192]{1,0:T(8,128)(2,1)}) custom-call(s32[2048]{0:T(1024)} %bitcast.39, bf16[2048,192]{1,0:T(8,128)(2,1)} %copy.47.refs_0_, bf16[2048,192]{1,0:T(8,128)(2,1)} %get-tuple-element.17.refs_1_, bf16[2048,192]{1,0:T(8,128)(2,1)} %copy.48.refs_2_, bf16[2048,192]{1,0:T(8,128)(2,1)} %copy.49.refs_3_, ...), custom_call_target="tpu_custom_call" | custom-call | tf_op jit(solution)/shard_map/rows/pallas_call | solution.py:78
  152.5 2.3 %copy.51 = bf16[1,2048,192]{1,2,0:T(8,128)(2,1)} copy(bf16[1,2048,192]{2,1,0:T(8,128)(2,1)} %bitcast.31) | data formatting | bytes 1572864
  154.7 1.2 copy.52
  156.0 0.8 copy.61
  156.7 0.3 copy-done.7
  157.1 0.7 copy.62
  157.8 0.6 copy.63
  (22 shorter events, 0.1 us)
Async XLA Ops:
  0.6 19.1 %collective-permute-start = (bf16[2048,192]{0,1:T(8,128)(2,1)}, bf16[2048,192]{0,1:T(8,128)(2,1)}, u32[]{:S(2)}, u32[]{:S(2)}) collective-permute-start(bf16[2048,192]{0,1:T(8,128)(2,1)} %bitcast.32), channel_id=1, source_target_pairs={{0,4},{4,8},{8,12},{12,16},{16,20},{20,24},{24,28},{28,32},{32,36}... | collective-permute-start | bytes 2359304 | tf_op jit(solution)/shard_map/ppermute | solution.py:420
  5.6 16.4 %collective-permute-start.1 = (bf16[2048,192]{0,1:T(8,128)(2,1)}, bf16[2048,192]{0,1:T(8,128)(2,1)}, u32[]{:S(2)}, u32[]{:S(2)}) collective-permute-start(bf16[2048,192]{0,1:T(8,128)(2,1)} %bitcast.33), channel_id=1, source_target_pairs={{4,0},{8,4},{12,8},{16,12},{20,16},{24,20},{28,24},{32,28},{36,32}... | collective-permute-start | bytes 2359304 | tf_op jit(solution)/shard_map/ppermute | solution.py:420
  8.0 16.2 %collective-permute-start.2 = (bf16[2048,192]{0,1:T(8,128)(2,1)}, bf16[2048,192]{0,1:T(8,128)(2,1)S(1)}, u32[]{:S(2)}, u32[]{:S(2)}) collective-permute-start(bf16[2048,192]{0,1:T(8,128)(2,1)} %bitcast.34), channel_id=1, source_target_pairs={{0,4},{4,8},{8,12},{12,16},{16,20},{20,24},{24,28},{28,32},{32,36}... | collective-permute-start | bytes 2359304 | tf_op jit(solution)/shard_map/ppermute | solution.py:420
  11.2 16.4 %collective-permute-start.3 = (bf16[2048,192]{0,1:T(8,128)(2,1)}, bf16[2048,192]{0,1:T(8,128)(2,1)S(1)}, u32[]{:S(2)}, u32[]{:S(2)}) collective-permute-start(bf16[2048,192]{0,1:T(8,128)(2,1)} %bitcast.35), channel_id=1, source_target_pairs={{4,0},{8,4},{12,8},{16,12},{20,16},{24,20},{28,24},{32,28},{36,32}... | collective-permute-start | bytes 2359304 | tf_op jit(solution)/shard_map/ppermute | solution.py:420
  13.1 2.3 %copy-start.4 = (bf16[1,2048,192]{1,2,0:T(8,128)(2,1)S(1)}, bf16[1,2048,192]{1,2,0:T(8,128)(2,1)}, u32[]{:S(2)}) copy-start(bf16[1,2048,192]{1,2,0:T(8,128)(2,1)} %param.9) | copy-start | bytes 2359300
  15.4 1.3 copy-start.6
  16.9 1.2 copy-start
  16.9 1.0 copy-start.8
  18.3 0.8 copy-start.2
  18.3 0.8 copy-start.9
  74.7 6.8 %copy-start.1 = (bf16[2048,192]{1,0:T(8,128)(2,1)S(1)}, bf16[2048,192]{1,0:T(8,128)(2,1)}, u32[]{:S(2)}) copy-start(bf16[2048,192]{1,0:T(8,128)(2,1)} %get-tuple-element.18.refs_4_) | copy-start | bytes 2359300
  76.3 60.9 %collective-permute-start.4 = (bf16[2048,192]{0,1:T(8,128)(2,1)S(1)}, bf16[2048,192]{0,1:T(8,128)(2,1)}, u32[]{:S(2)}, u32[]{:S(2)}) collective-permute-start(bf16[2048,192]{0,1:T(8,128)(2,1)S(1)} %copy.43), channel_id=1, source_target_pairs={{0,4},{4,8},{8,12},{12,16},{16,20},{20,24},{24,28},{28,32},{32,36}... | collective-permute-start | bytes 2359304 | tf_op jit(solution)/shard_map/ppermute | solution.py:420
  78.2 61.1 %collective-permute-start.5 = (bf16[2048,192]{0,1:T(8,128)(2,1)S(1)}, bf16[2048,192]{0,1:T(8,128)(2,1)S(1)}, u32[]{:S(2)}, u32[]{:S(2)}) collective-permute-start(bf16[2048,192]{0,1:T(8,128)(2,1)S(1)} %copy.43), channel_id=1, source_target_pairs={{4,0},{8,4},{12,8},{16,12},{20,16},{24,20},{28,24},{32,28},{36,32}... | collective-permute-start | bytes 2359304 | tf_op jit(solution)/shard_map/ppermute | solution.py:420
  81.5 5.7 %copy-start.10 = (s32[1,2048]{1,0:T(1,128)S(1)}, s32[1,2048]{1,0:T(1,128)}, u32[]{:S(2)}) copy-start(s32[1,2048]{1,0:T(1,128)} %param.13) | copy-start | bytes 24580
  82.0 58.6 %collective-permute-start.6 = (bf16[2048,192]{0,1:T(8,128)(2,1)S(1)}, bf16[2048,192]{0,1:T(8,128)(2,1)}, u32[]{:S(2)}, u32[]{:S(2)}) collective-permute-start(bf16[2048,192]{0,1:T(8,128)(2,1)S(1)} %copy.45), channel_id=1, source_target_pairs={{0,4},{4,8},{8,12},{12,16},{16,20},{20,24},{24,28},{28,32},{32,36}... | collective-permute-start | bytes 2359304 | tf_op jit(solution)/shard_map/ppermute | solution.py:420
  84.6 58.2 %collective-permute-start.7 = (bf16[2048,192]{0,1:T(8,128)(2,1)S(1)}, bf16[2048,192]{0,1:T(8,128)(2,1)S(1)}, u32[]{:S(2)}, u32[]{:S(2)}) collective-permute-start(bf16[2048,192]{0,1:T(8,128)(2,1)S(1)} %copy.45), channel_id=1, source_target_pairs={{4,0},{8,4},{12,8},{16,12},{20,16},{24,20},{28,24},{32,28},{36,32}... | collective-permute-start | bytes 2359304 | tf_op jit(solution)/shard_map/ppermute | solution.py:420
  152.5 2.3 %copy-start.3 = (bf16[2048,192]{1,0:T(8,128)(2,1)S(1)}, bf16[2048,192]{1,0:T(8,128)(2,1)}, u32[]{:S(2)}) copy-start(bf16[2048,192]{1,0:T(8,128)(2,1)} %get-tuple-element.20) | copy-start | bytes 2359300
  154.7 1.2 copy-start.5
  156.0 1.1 copy-start.7
  157.1 0.7 copy-start.11

commit v2 on v0

v2 whole, which is shorter than its diff:
```python
import jax
import jax.numpy as jnp
from jax import lax
from jax.experimental import pallas as pl
from jax.experimental.pallas import tpu as pltpu
from jax.sharding import PartitionSpec as P

HEADS = 3
PATCH = 1024
PATCHES = 2
C = 192
D = 64
LANES = 128
N = 2048
QB = 256
EPS = 1e-5
LOG2E = 1.4426950408889634
BF = jnp.bfloat16
F32 = jnp.float32
MESH = pl.DeviceIdType.MESH
VMEM_LIMIT = 62 * 2**20
PLANE = 32
DEPTH = 8
TILES = 5
UNROLL = 16


def dot(a, b):
    return jnp.dot(a, b, preferred_element_type=F32)


def dot_nt(a, b):
    return lax.dot_general(a, b, (((1,), (1,)), ((), ())), preferred_element_type=F32)


def turned(a):
    return a.astype(F32).T.astype(a.dtype)


SCRATCH = dict(
    x_in=((C, N), BF), g_in=((C, N), BF),
    x_ext=((2, C, N), BF), g_ext=((2, C, N), BF),
    y_ext=((2, PATCHES, C, PATCH), BF), dx_ext=((2, PATCHES, C, PATCH), BF),
    x_hil=((PATCHES, C, PATCH), BF), g_hil=((PATCHES, C, PATCH), BF),
    y_hil=((PATCHES, C, PATCH), BF), dx_hil=((PATCHES, C, PATCH), BF),
    src=((4 * N * 2, LANES), F32), dst=((N * 2, LANES), F32),
    gain=((C, LANES), F32), w_qkv_t=((3 * C, C), BF), w_proj_t=((C, C), BF),
    inv=((PATCHES, 1, PATCH), F32), unit=((PATCHES, C, PATCH), F32),
    normed=((PATCHES, C, PATCH), BF), g_live=((PATCHES, C, PATCH), BF),
    q_ext=((HEADS, 2 * D, PATCH), BF), q_row=((HEADS, PATCH, D), BF),
    k_t=((HEADS, D, PATCH), BF), k_ext=((HEADS, PATCH, 2 * D), BF),
    v_t=((HEADS, D, PATCH), BF), v_row=((HEADS, PATCH, D), BF),
    do_t=((HEADS, D, PATCH), BF), do_row=((HEADS, PATCH, D), BF),
    attn=((PATCHES, C, PATCH), BF), d_qkv=((PATCHES, 3 * C, PATCH), BF),
    dk=((HEADS, PATCH, D), F32), dv=((HEADS, PATCH, D), F32),
    gq=((C, 3 * C), F32), gp=((C, C), F32),
    tot=((PLANE, TILES, 8, LANES), F32), recv_a=((PLANE, TILES, 8, LANES), F32),
    recv_z=((DEPTH, TILES, 8, LANES), F32), all_a=((PLANE, TILES, 8, LANES), F32),
)
SEMS = dict(
    in_sem=(2,), x_s=(2,), x_r=(2,), g_s=(2,), g_r=(2,),
    y_s=(2, PATCHES), y_r=(2, PATCHES), dx_s=(2, PATCHES), dx_r=(2, PATCHES),
    a_s=(PLANE,), a_r=(PLANE,), z_s=(DEPTH,), z_r=(DEPTH,), c_s=(PLANE,), c_r=(PLANE,),
)


class Refs:
    pass


def loop(lo, hi, f):
    def body(i, c):
        f(i)
        return c

    lax.fori_loop(lo, hi, body, 0)


def fill(r, at, cols):
    n = cols.shape[1]
    at = pl.multiple_of(at, n)
    cols = cols.astype(F32)
    r.src[pl.ds(2 * at, n, stride=2), :] = cols[:LANES].T
    tail = jnp.concatenate([cols[LANES:], jnp.zeros((2 * LANES - C, n), F32)], axis=0)
    r.src[pl.ds(2 * at + 1, n, stride=2), :] = tail.T


def fill_all(r, at, ref):
    def piece(t):
        fill(r, at + t * 512, ref[:, pl.ds(pl.multiple_of(t * 512, 512), 512)])

    loop(0, ref.shape[1] // 512, piece)


def pick(r, idx_ref):
    def rows(t):
        for u in range(UNROLL):
            j = t * UNROLL + u
            r.dst[pl.ds(pl.multiple_of(2 * j, 2), 2), :] = r.src[pl.ds(idx_ref[j], 2), :]

    loop(0, N // UNROLL, rows)


def picked(r, at, n):
    head = r.dst[pl.ds(2 * at, n, stride=2), :].T
    tail = r.dst[pl.ds(2 * at + 1, n, stride=2), :].T
    return jnp.concatenate([head, tail[: C - LANES]], axis=0).astype(BF)


def live_lanes(live_n):
    return lax.broadcasted_iota(jnp.int32, (1, PATCH), 1) < live_n


def prep_x(r, p):
    x = r.x_hil[p].astype(F32)
    center = x - jnp.mean(x, axis=0, keepdims=True)
    inv = lax.rsqrt(jnp.mean(center * center, axis=0, keepdims=True) + EPS)
    unit = center * inv
    r.inv[p] = inv
    r.unit[p] = unit
    r.normed[p] = (unit * r.gain[:, :1]).astype(BF)


def prep_heads(r, p, live_n):
    nm = r.normed[p]
    live = live_lanes(live_n)
    gl = jnp.where(live, r.g_hil[p].astype(F32), 0.0).astype(BF)
    r.g_live[p] = gl
    first = lax.broadcasted_iota(jnp.int32, (D, PATCH), 0) == 0
    bias = jnp.where(first, jnp.where(live, 0.0, -1e30), 0.0)
    ones = jnp.where(first, 1.0, 0.0).astype(BF)
    q = dot(r.w_qkv_t[:C, :], nm).astype(BF).astype(F32) * 0.125
    k = dot(r.w_qkv_t[C : 2 * C, :], nm).astype(BF).astype(F32)
    v = dot(r.w_qkv_t[2 * C :, :], nm).astype(BF).astype(F32)
    do = dot(r.w_proj[...], gl).astype(BF).astype(F32)
    for h in range(HEADS):
        hs = slice(h * D, (h + 1) * D)
        r.q_ext[h, :D, :] = q[hs].astype(BF)
        r.q_ext[h, D:, :] = ones
        r.q_row[h] = q[hs].T.astype(BF)
        r.k_t[h] = k[hs].astype(BF)
        r.k_ext[h] = jnp.concatenate([k[hs], bias], axis=0).T.astype(BF)
        r.v_t[h] = v[hs].astype(BF)
        r.v_row[h] = v[hs].T.astype(BF)
        r.do_t[h] = do[hs].astype(BF)
        r.do_row[h] = do[hs].T.astype(BF)


def core(r, p):
    blocks = PATCH // QB
    steps = [(h, b) for h in range(HEADS) for b in range(blocks)]

    def scores(i):
        h, b = steps[i]
        cs = slice(b * QB, (b + 1) * QB)
        return dot(r.k_ext[h], r.q_ext[h, :, cs]), dot(r.v_row[h], r.do_t[h, :, cs])

    def softmax(i, pair):
        h, b = steps[i]
        cs = slice(b * QB, (b + 1) * QB)
        s, dp = pair
        m = jnp.max(s, axis=0, keepdims=True)
        e = jnp.exp2((s - m) * LOG2E)
        pn = e * (1.0 / jnp.sum(e, axis=0, keepdims=True))
        pb = pn.astype(BF)
        o = dot(r.v_t[h], pb)
        r.attn[p, h * D : (h + 1) * D, cs] = o.astype(BF)
        delta = jnp.sum(o * r.do_t[h, :, cs].astype(F32), axis=0, keepdims=True)
        return pb, (pn * (dp - delta)).astype(BF)

    def grads(i, pair):
        h, b = steps[i]
        cs = slice(b * QB, (b + 1) * QB)
        pb, ds = pair
        r.d_qkv[p, h * D : (h + 1) * D, cs] = (dot(r.k_t[h], ds) * 0.125).astype(BF)
        dk = dot(ds, r.q_row[h, cs, :])
        dv = dot(pb, r.do_row[h, cs, :])
        if b:
            dk = r.dk[h] + dk
            dv = r.dv[h] + dv
        if b < blocks - 1:
            r.dk[h] = dk
            r.dv[h] = dv
        else:
            r.d_qkv[p, C + h * D : C + (h + 1) * D, :] = dk.T.astype(BF)
            r.d_qkv[p, 2 * C + h * D : 2 * C + (h + 1) * D, :] = dv.T.astype(BF)

    ahead = scores(0)
    behind = None
    for i in range(len(steps)):
        now = ahead
        ahead = scores(i + 1) if i + 1 < len(steps) else None
        pair = softmax(i, now)
        if behind is not None:
            grads(i - 1, behind)
        behind = pair
    grads(len(steps) - 1, behind)


def weight_grads(r, p):
    return dot_nt(r.normed[p], r.d_qkv[p]), dot_nt(r.attn[p], r.g_live[p])


def block_rows(r, p, live_n):
    livef = jnp.where(live_lanes(live_n), 1.0, 0.0)
    branch = dot(r.w_proj_t[...], r.attn[p])
    r.y_hil[p] = (r.x_hil[p].astype(F32) + livef * branch).astype(BF)


def feature_grads(r, p):
    du = dot(r.w_qkv[...], r.d_qkv[p]) * r.gain[:, :1]
    unit = r.unit[p]
    dr = r.inv[p] * (
        du
        - jnp.mean(du, axis=0, keepdims=True)
        - unit * jnp.mean(du * unit, axis=0, keepdims=True)
    )
    r.dx_hil[p] = (r.g_hil[p].astype(F32) + dr).astype(BF)


def kernel(
    cnt_ref, zor_ref, hil_ref, x_hbm, g_hbm, gain_ref, wqkv_ref, wproj_ref,
    y_ref, dx_ref, gqkv_ref, gproj_ref, ggain_ref, *scratch,
):
    r = Refs()
    for name, ref in zip(list(SCRATCH) + list(SEMS), scratch):
        setattr(r, name, ref)
    r.w_qkv, r.w_proj = wqkv_ref, wproj_ref
    seq = lax.axis_index("seq")
    x_at = lax.axis_index("dp")
    last = lax.axis_size("seq") - 1
    y_at = seq // 16
    z_at = (seq // 2) % 8
    core_at = seq % 2
    a = (y_at * 4 + x_at) * 2 + core_at
    home = (seq % 4) * N
    sides = (((seq + 3) % 4) * N, ((seq + 1) % 4) * N)

    def plane(o):
        return {"dp": (o // 2) % 4, "seq": (o // 8) * 16 + z_at * 2 + o % 2}

    def depth(o):
        return {"dp": x_at, "seq": y_at * 16 + o * 2 + core_at}

    barrier = pltpu.get_barrier_semaphore()

    def greet(dev):
        pl.semaphore_signal(barrier, inc=1, device_id=dev, device_id_type=MESH)

    has_left = seq > 0
    has_right = seq < last

    @pl.when(has_left)
    def _():
        greet({"seq": seq - 1})

    @pl.when(has_right)
    def _():
        greet({"seq": seq + 1})

    loop(1, PLANE, lambda i: greet(plane((a + i) % PLANE)))
    loop(1, DEPTH, lambda i: greet(depth((z_at + i) % DEPTH)))

    x_copy = pltpu.make_async_copy(x_hbm, r.x_in, r.in_sem.at[0])
    g_copy = pltpu.make_async_copy(g_hbm, r.g_in, r.in_sem.at[1])
    x_copy.start()
    g_copy.start()
    peers = PLANE - 1 + DEPTH - 1
    inner = jnp.logical_and(has_left, has_right)

    @pl.when(inner)
    def _():
        pl.semaphore_wait(barrier, peers + 2)

    @pl.when(jnp.logical_not(inner))
    def _():
        pl.semaphore_wait(barrier, peers + 1)

    def to_left(ref, ext, ss, rs, *at):
        return pltpu.make_async_remote_copy(
            ref, ext.at[(1,) + at], ss.at[(1,) + at], rs.at[(1,) + at],
            device_id={"seq": seq - 1}, device_id_type=MESH,
        )

    def to_right(ref, ext, ss, rs, *at):
        return pltpu.make_async_remote_copy(
            ref, ext.at[(0,) + at], ss.at[(0,) + at], rs.at[(0,) + at],
            device_id={"seq": seq + 1}, device_id_type=MESH,
        )

    def send(*args):
        @pl.when(has_left)
        def _():
            to_left(*args).start()

        @pl.when(has_right)
        def _():
            to_right(*args).start()

    def received(ref, ext, ss, rs, *at):
        def arrival(slot, peer):
            return pltpu.make_async_remote_copy(
                ref, ext.at[(slot,) + at], ss.at[(slot,) + at], rs.at[(slot,) + at],
                device_id={"seq": peer}, device_id_type=MESH,
            )

        @pl.when(has_left)
        def _():
            arrival(0, seq - 1).wait_recv()

        @pl.when(has_right)
        def _():
            arrival(1, seq + 1).wait_recv()

    def sent(*args):
        @pl.when(has_left)
        def _():
            to_left(*args).wait_send()

        @pl.when(has_right)
        def _():
            to_right(*args).wait_send()

    x_args = (x_hbm, r.x_ext, r.x_s, r.x_r)
    g_args = (g_hbm, r.g_ext, r.g_s, r.g_r)

    def y_args(p):
        return (r.y_hil.at[p], r.y_ext, r.y_s, r.y_r, p)

    def dx_args(p):
        return (r.dx_hil.at[p], r.dx_ext, r.dx_s, r.dx_r, p)

    send(*x_args)
    r.w_qkv_t[...] = turned(wqkv_ref[...])
    r.w_proj_t[...] = turned(wproj_ref[...])
    r.gain[...] = jnp.broadcast_to(gain_ref[...], (LANES, C)).T
    x_copy.wait()
    g_copy.wait()
    fill_all(r, home, r.x_in)
    received(*x_args)
    send(*g_args)
    fill_all(r, sides[0], r.x_ext.at[0])
    fill_all(r, sides[1], r.x_ext.at[1])
    pick(r, zor_ref)

    def take_x(p):
        r.x_hil[p] = picked(r, p * PATCH, PATCH)
        prep_x(r, p)

    loop(0, PATCHES, take_x)
    fill_all(r, home, r.g_in)
    received(*g_args)
    fill_all(r, sides[0], r.g_ext.at[0])
    fill_all(r, sides[1], r.g_ext.at[1])
    pick(r, zor_ref)

    def take_g(p):
        r.g_hil[p] = picked(r, p * PATCH, PATCH)

    loop(0, PATCHES, take_g)

    prep_heads(r, 0, cnt_ref[0])
    core(r, 0)
    gq, gp = weight_grads(r, 0)
    r.gq[...] = gq
    r.gp[...] = gp
    block_rows(r, 0, cnt_ref[0])
    send(*y_args(0))
    feature_grads(r, 0)
    send(*dx_args(0))

    prep_heads(r, 1, cnt_ref[1])
    core(r, 1)
    gq, gp = weight_grads(r, 1)
    whole = jnp.concatenate([r.gq[...] + gq, r.gp[...] + gp], axis=1)
    for rt in range(C // 8):
        for ct in range(6):
            t = rt * 6 + ct
            r.tot[t // TILES, t % TILES, :, :] = whole[
                rt * 8 : (rt + 1) * 8, ct * LANES : (ct + 1) * LANES
            ]
    for t in range(144, PLANE * TILES):
        r.tot[t // TILES, t % TILES, :, :] = jnp.zeros((8, LANES), F32)

    def copy_a(o):
        return pltpu.make_async_remote_copy(
            r.tot.at[o], r.recv_a.at[a], r.a_s.at[o], r.a_r.at[a],
            device_id=plane(o), device_id_type=MESH,
        )

    def into_a(o):
        return pltpu.make_async_remote_copy(
            r.tot.at[o], r.recv_a.at[o], r.a_s.at[o], r.a_r.at[o],
            device_id=plane(o), device_id_type=MESH,
        )

    def copy_z(o):
        return pltpu.make_async_remote_copy(
            r.recv_z.at[z_at], r.recv_z.at[z_at], r.z_s.at[o], r.z_r.at[z_at],
            device_id=depth(o), device_id_type=MESH,
        )

    def into_z(o):
        return pltpu.make_async_remote_copy(
            r.recv_z.at[o], r.recv_z.at[o], r.z_s.at[o], r.z_r.at[o],
            device_id=depth(o), device_id_type=MESH,
        )

    def copy_c(o):
        return pltpu.make_async_remote_copy(
            r.all_a.at[a], r.all_a.at[a], r.c_s.at[o], r.c_r.at[a],
            device_id=plane(o), device_id_type=MESH,
        )

    def into_c(o):
        return pltpu.make_async_remote_copy(
            r.all_a.at[o], r.all_a.at[o], r.c_s.at[o], r.c_r.at[o],
            device_id=plane(o), device_id_type=MESH,
        )

    def in_plane(f):
        loop(1, PLANE, lambda i: f((a + i) % PLANE))

    def in_depth(f):
        loop(1, DEPTH, lambda i: f((z_at + i) % DEPTH))

    in_plane(lambda o: copy_a(o).start())
    r.recv_a[a] = r.tot[a]

    block_rows(r, 1, cnt_ref[1])
    send(*y_args(1))
    feature_grads(r, 1)
    send(*dx_args(1))

    def own(ref):
        fill(r, home, ref[0])
        fill(r, home + PATCH, ref[1])

    def side(slot, ext, p):
        fill(r, sides[slot] + p * PATCH, ext[slot, p])

    received(*y_args(0))
    own(r.y_hil)
    side(0, r.y_ext, 0)
    side(1, r.y_ext, 0)

    in_plane(lambda o: into_a(o).wait_recv())
    acc = r.recv_a[0]
    for i in range(1, PLANE):
        acc = acc + r.recv_a[i]
    r.recv_z[z_at] = acc
    in_depth(lambda o: copy_z(o).start())

    received(*y_args(1))
    side(0, r.y_ext, 1)
    side(1, r.y_ext, 1)
    pick(r, hil_ref)

    in_depth(lambda o: into_z(o).wait_recv())
    acc = r.recv_z[0]
    for i in range(1, DEPTH):
        acc = acc + r.recv_z[i]
    r.all_a[a] = acc
    in_plane(lambda o: copy_c(o).start())

    def put(ref):
        def piece(t):
            at = pl.multiple_of(t * 512, 512)
            ref[:, pl.ds(at, 512)] = picked(r, t * 512, 512)

        loop(0, N // 512, piece)

    put(y_ref)
    received(*dx_args(0))
    received(*dx_args(1))
    own(r.dx_hil)
    for p in range(PATCHES):
        side(0, r.dx_ext, p)
        side(1, r.dx_ext, p)
    pick(r, hil_ref)
    put(dx_ref)

    in_plane(lambda o: into_c(o).wait_recv())

    def tile(rt, ct):
        t = rt * 6 + ct
        return r.all_a[t // TILES, t % TILES, :, :]

    for rt in range(C // 8):
        rows = slice(rt * 8, (rt + 1) * 8)
        for ct in range(4):
            gqkv_ref[rows, ct * LANES : (ct + 1) * LANES] = tile(rt, ct)
        mid = tile(rt, 4)
        gqkv_ref[rows, 4 * LANES :] = mid[:, :D]
        gproj_ref[rows, :] = jnp.concatenate([mid[:, D:], tile(rt, 5)], axis=1)
    gg = jnp.sum(gqkv_ref[...] * wqkv_ref[...].astype(F32), axis=1, keepdims=True)
    gg = jnp.broadcast_to(gg, (C, LANES)) / r.gain[...]
    ggain_ref[...] = gg.T[:1, :]

    sent(*x_args)
    sent(*g_args)
    for p in range(PATCHES):
        sent(*y_args(p))
        sent(*dx_args(p))
    in_plane(lambda o: copy_a(o).wait_send())
    in_depth(lambda o: copy_z(o).wait_send())
    in_plane(lambda o: copy_c(o).wait_send())


def place(index):
    return (index[0] % (4 * N)) * 2


def hand_out(*refs):
    for i in range(5):
        refs[5 + i][...] = refs[i][...]


def shards(features, grad_out, norm_gain, w_qkv, w_proj, to_hilbert, to_zorder, counts):
    vmem = pl.BlockSpec(memory_space=pltpu.VMEM)
    smem = pl.BlockSpec(memory_space=pltpu.SMEM)
    hbm = pl.BlockSpec(memory_space=pl.ANY)
    made = pl.pallas_call(
        kernel,
        out_shape=(
            jax.ShapeDtypeStruct((C, N), BF),
            jax.ShapeDtypeStruct((C, N), BF),
            jax.ShapeDtypeStruct((C, 3 * C), F32),
            jax.ShapeDtypeStruct((C, C), F32),
            jax.ShapeDtypeStruct((1, C), F32),
        ),
        in_specs=[smem, smem, smem, hbm, hbm, vmem, vmem, vmem],
        out_specs=(vmem,) * 5,
        scratch_shapes=[pltpu.VMEM(s, d) for s, d in SCRATCH.values()]
        + [pltpu.SemaphoreType.DMA(s) for s in SEMS.values()],
        compiler_params=pltpu.CompilerParams(
            collective_id=0, has_side_effects=True, vmem_limit_bytes=VMEM_LIMIT
        ),
        name="block",
    )(
        counts[0], place(to_zorder), place(to_hilbert), features[0].T, grad_out[0].T,
        norm_gain.reshape(1, C), w_qkv, w_proj,
    )
    y, dx, gqkv, gproj, ggain = pl.pallas_call(
        hand_out,
        out_shape=[jax.ShapeDtypeStruct(m.shape, m.dtype) for m in made],
        in_specs=[vmem] * 5,
        out_specs=[vmem] * 5,
        name="hand_out",
    )(*made)
    return (y.T[None], dx.T[None], gqkv, gproj, ggain[0])


def solution(mesh):
    rows = P("dp", "seq", None)
    in_specs = (rows, rows, P(), P(), P(), P("dp", "seq"), P("dp", "seq"), P("dp", "seq"))
    out_specs = (rows, rows, P(), P(), P())
    return jax.shard_map(shards, mesh=mesh, in_specs=in_specs, out_specs=out_specs, check_vma=False)
```

time: 588 us -> 104 us (0.18)
  matrix products: 154 us -> 0 us
  waiting for transfers between devices: 151 us -> 0 us
  local copies, waits for them, and re-layouts: 114 us -> 0.69 us
  Pallas kernels: 0 us -> 101 us
  blocking collectives: 85.9 us -> 0 us
  other arithmetic: 41 us -> 1.31 us
  starting transfers between devices: 23.5 us -> 0 us
  between operations: 17 us -> 0.65 us
    psum x1 -> x0, waiting for transfers between devices: 150 us -> none  [shards(): lax.psum((local_totals[0], local_totals[1], local_totals[2]), ('seq', 'dp'))]
    dot_general x22 -> x0, matrix products: 124 us -> none  [the longest x2 36.8 us: patch_backward(): jnp.einsum('hqk,khd->qhd', d_scores, keys_h, preferred_element_type=jnp.f...]
    pallas_call x0 -> x2, Pallas kernels: none -> 101 us  [the longest x1 98.2 us: shards(): pl.pallas_call(kernel, out_shape=(jax.ShapeDtypeStruct((C, N), BF), jax.S...]
    psum x1 -> x0, blocking collectives: 85.9 us -> none  [shards(): lax.psum((local_totals[0], local_totals[1], local_totals[2]), ('seq', 'dp'))]
    gather x8 -> x0, local copies, waits for them, and re-layouts: 63.2 us -> none  [the longest x2 16.8 us: shards(): dx_zor = extended(dx_hil[send_back], (('seq', 0),), spill)[place_back]]
    sub x4 -> x0, matrix products: 30.1 us -> none  [probabilities(): weights = jnp.exp(scores - highest)]
    ppermute x8 -> x0, starting transfers between devices: 23.5 us -> none  [the longest x4 15.4 us: extended(): before = lax.ppermute(last, axis, up)]
    sort x4 -> x0, other arithmetic: 20.9 us -> none  [the longest x2 10.8 us: route_plan(): send_order = jnp.argsort(send_key, stable=True)]
  transfers between devices with their start and end apart: 9 -> 0, of which waited for: 1 -> 0; matrix products, arithmetic and copies ran while one was open for 22% -> 0% of each run, Pallas kernels for 0% -> 0%
where the time goes in v2:
time: 104 us
  Pallas kernels  101 us (97%)
  other arithmetic  1.31 us (1%)
    pallas_call x1, Pallas kernels, shards(): pl.pallas_call(kernel, out_shape=(jax.ShapeDtypeStruct((C, N), BF), jax.S...  98.2 us
    pallas_call x1, Pallas kernels, shards(): pl.pallas_call(hand_out, out_shape=[jax.ShapeDtypeStruct(m.shape, m.dtype...  2.98 us

profile of v2, /device:TPU:1, one launch (start us, length us, event | category | flops | bytes accessed | tf_op | source)
XLA Modules:
  0.0 103.8 jit_solution(13889514326945958417)
XLA Ops:
  0.6 0.0 copy-start
  0.6 0.7 copy-done
  1.3 1.3 %fusion.1 = (s32[2048]{0:T(1024)}, s32[2048]{0:T(1024)}) fusion(s32[2048]{0:T(1024)S(1)} %bitcast.19, s32[2048]{0:T(1024)} %bitcast.20), kind=kLoop, calls=%fused_computation.7 | loop fusion | flops 49152 | bytes 32768 | tf_op jit(solution)/shard_map/mul | solution.py:511
  2.6 98.2 %block.1 = (bf16[192,2048]{1,0:T(8,128)(2,1)}, bf16[192,2048]{1,0:T(8,128)(2,1)}, f32[192,576]{1,0:T(8,128)}, f32[192,192]{1,0:T(8,128)}, f32[1,192]{1,0:T(1,128)}) custom-call(s32[2]{0:T(128)} %bitcast.22, s32[2048]{0:T(1024)} %get-tuple-element.25.zor_ref, s32[2048]{0:T(1024)} %get-tuple-element.26.hil_ref, bf16[192,2048]{1,0:T(8,128)(2,1)} %bitcast.17, ...), custom_call_target="tpu_custom_call" | custom-call | tf_op jit(solution)/shard_map/block/pallas_call | solution.py:523
  100.8 3.0 %hand_out.1 = (bf16[192,2048]{1,0:T(8,128)(2,1)}, bf16[192,2048]{1,0:T(8,128)(2,1)}, f32[192,576]{1,0:T(8,128)}, f32[192,192]{1,0:T(8,128)}, f32[1,192]{1,0:T(1,128)}) custom-call(bf16[192,2048]{1,0:T(8,128)(2,1)} %get-tuple-element.15.refs_0_, bf16[192,2048]{1,0:T(8,128)(2,1)} %get-tuple-element.16.refs_1_, f32[192,576]{1,0:T(8,128)} %get-tuple-element.17.refs_2_, ...), custom_call_target="tpu_custom_call" | custom-call | tf_op jit(solution)/shard_map/hand_out/pallas_call | solution.py:544
Async XLA Ops:
  0.6 0.7 copy-start
